TPU v7x, 512 devices: a whole 4x4x16 slice. The times are simulated.
512 devices in a mesh: row: 16 (over x_lo, y, core), col: 32 (over x_hi, z).
Axes of the slice: x: 4 (x_hi: 2, x_lo: 2; x = x_hi * 2 + x_lo), y: 4, z: 16, core: 2. Of those that a mesh axis runs over, the one named last changes fastest.
Arguments:
- coarse_blocks: bfloat16 [16, 32, 2, 20, 128], P('row', 'col'), may hold values from -18 to 18
- block_ids: int32 [16, 32, 6], P('row', 'col'), may hold values from 0 to 1023, as said below
- quadrant: int32 [16, 32, 6], P('row', 'col'), may hold values from 0 to 1
- land_mask: int32 [512, 1024], P('row', 'col'), may hold values from 0 to 1
- lift_weight: bfloat16 [20, 128], replicated, may hold values from -1.25 to 1.25
- land_vector: float32 [128], replicated, may hold values from -6 to 6
- norm_gain: float32 [128], replicated, may hold values from 0.5 to 2
- first_weight: bfloat16 [9, 128, 128], replicated, may hold values from -0.1875 to 0.1875
- second_weight: bfloat16 [9, 128, 128], replicated, may hold values from -0.1875 to 0.1875
- cotangent: bfloat16 [512, 1024, 128], P('row', 'col'), may hold values from -6 to 6
Outputs:
- features: bfloat16 [512, 1024, 128], P('row', 'col')
- grad_coarse: float32 [16, 32, 2, 20, 128], P('row', 'col')
- grad_first: float32 [9, 128, 128], replicated
- grad_second: float32 [9, 128, 128], replicated
- grad_lift: float32 [20, 128], replicated
- grad_land: float32 [128], replicated
- grad_gain: float32 [128], replicated
Inputs may be any that keep to these rules, and one draw needn't show every extreme that they name: `block_ids`: each entry names a block whose owning tile lies at most one tile away along the rows and along the columns (diagonals included) from the listing tile; the first entry of each list names a block of the listing tile itself.
All inputs are finite; a program needn't handle non-finite values.
Results may differ from a plain program's by a relative error of at most 0.005.
Values may be sent and summed in bfloat16 or wider, within the bound.
A program may use at most 64 MiB of HBM per device.

v0:
```python
import math

import jax
import jax.numpy as jnp
from jax import lax
from jax.sharding import PartitionSpec as P

GROUPS = 32


EPSILON = 1e-05
PRECISE = lax.Precision.HIGHEST


def extended(x, sides, width):
    for axis, dim in sides:
        devices, length = (lax.axis_size(axis), x.shape[dim])
        up = [(i, (i + 1) % devices) for i in range(devices - 1)]
        down = [(j, i) for i, j in up]
        last = lax.slice_in_dim(x, length - width, length, axis=dim)
        leading = lax.slice_in_dim(x, 0, width, axis=dim)
        before = lax.ppermute(last, axis, up)
        after = lax.ppermute(leading, axis, down)
        x = jnp.concatenate([before, x, after], axis=dim)
    return x


def shifted(x, axis, by):
    devices = lax.axis_size(axis)
    pairs = [(i, i + by) for i in range(devices) if 0 <= i + by < devices]
    return lax.ppermute(x, axis, pairs)


def upsample_matrix(fine_len, coarse_len):
    position = jnp.arange(fine_len, dtype=jnp.float32)
    location = jnp.clip((position + 0.5) / 2.0 - 0.5, 0.0, coarse_len - 1.0)
    lower = jnp.floor(location)
    fraction = location - lower
    lower_idx = lower.astype(jnp.int32)
    upper_idx = jnp.minimum(lower_idx + 1, coarse_len - 1)
    columns = jnp.arange(coarse_len, dtype=jnp.int32)
    low_part = (columns[None, :] == lower_idx[:, None]).astype(jnp.float32)
    high_part = (columns[None, :] == upper_idx[:, None]).astype(jnp.float32)
    return (1.0 - fraction)[:, None] * low_part + fraction[:, None] * high_part


def apply_taps(padded, weight, row_count, col_count, flipped):
    channels = padded.shape[2]
    summed = jnp.zeros((row_count * col_count, weight.shape[2]), jnp.float32)
    for number in range(9):
        row_off, col_off = divmod(number, 3)
        if flipped:
            window = padded[
                2 - row_off : 2 - row_off + row_count, 2 - col_off : 2 - col_off + col_count
            ]
            summed = summed + jnp.dot(
                window.reshape(-1, channels), weight[number].T, preferred_element_type=jnp.float32
            )
        else:
            window = padded[row_off : row_off + row_count, col_off : col_off + col_count]
            summed = summed + jnp.dot(
                window.reshape(-1, channels), weight[number], preferred_element_type=jnp.float32
            )
    return summed


def tap_grads(padded, grads, row_count, col_count):
    channels = padded.shape[2]
    stacked = []
    for number in range(9):
        row_off, col_off = divmod(number, 3)
        window = padded[row_off : row_off + row_count, col_off : col_off + col_count].reshape(
            -1, channels
        )
        stacked.append(
            lax.dot_general(
                window, grads, (((0,), (0,)), ((), ())), preferred_element_type=jnp.float32
            )
        )
    return jnp.stack(stacked)


def silu_slope(values):
    gate_part = jax.nn.sigmoid(values)
    return gate_part * (1.0 + values * (1.0 - gate_part))


def with_rim(image):
    return extended(image, (("row", 0), ("col", 1)), 1)


def shards(
    coarse_blocks,
    block_ids,
    quadrant,
    land_mask,
    lift_weight,
    land_vector,
    norm_gain,
    first_weight,
    second_weight,
    cotangent,
):
    row_devices = lax.axis_size("row")
    col_devices = lax.axis_size("col")
    row_place = lax.axis_index("row")
    col_place = lax.axis_index("col")
    blocks_here = coarse_blocks.shape[2]
    in_channels = coarse_blocks.shape[3]
    tile_rows, tile_cols, channels = cotangent.shape
    half_rows = tile_rows // 2
    coarse_rows = tile_rows // 4
    coarse_cols = tile_cols // 2
    pixels = tile_rows * tile_cols
    block_width = in_channels * coarse_rows * coarse_cols
    per_group = channels // GROUPS
    members = float(row_devices * tile_rows * col_devices * tile_cols * per_group)
    report = 1.0 / math.sqrt(row_devices * tile_rows * col_devices * tile_cols)
    beside_all = extended(coarse_blocks, (("row", 0), ("col", 1)), 1)
    candidates = beside_all.reshape(9 * blocks_here, block_width)
    block_list = block_ids.reshape(-1)
    owner_id = block_list // blocks_here
    member = block_list % blocks_here
    slot_index = (
        (owner_id // col_devices - row_place + 1) * 3 + (owner_id % col_devices - col_place + 1)
    ) * blocks_here + member
    slot_hot = (
        slot_index[:, None] == jnp.arange(9 * blocks_here, dtype=jnp.int32)[None, :]
    ).astype(jnp.float32)
    half_hot = (quadrant.reshape(-1)[:, None] == jnp.arange(2, dtype=jnp.int32)[None, :]).astype(
        jnp.float32
    )
    selector = jnp.dot(half_hot.T, slot_hot, precision=PRECISE)
    block_sums = jnp.dot(
        selector.astype(jnp.bfloat16), candidates, preferred_element_type=jnp.float32
    )
    row_up = upsample_matrix(half_rows, coarse_rows)
    col_up = upsample_matrix(tile_cols, coarse_cols)
    coarse_grid = block_sums.reshape(2, in_channels, coarse_rows, coarse_cols)
    upsampled = jnp.einsum("ia,qhab,jb->hqij", row_up, coarse_grid, col_up, precision=PRECISE)
    fine_input = upsampled.reshape(in_channels, pixels).astype(jnp.bfloat16)
    land_float = land_mask.reshape(-1).astype(jnp.float32)
    lifted = (
        jnp.einsum("hp,hd->pd", fine_input, lift_weight, preferred_element_type=jnp.float32)
        + land_float[:, None] * land_vector[None, :]
    )
    grouped = lifted.reshape(pixels, GROUPS, per_group)
    group_total = lax.psum(jnp.sum(grouped, axis=(0, 2)), ("row", "col"))
    group_mean = group_total / members
    centered = grouped - group_mean[None, :, None]
    variance = lax.psum(jnp.sum(centered * centered, axis=(0, 2)), ("row", "col")) / members
    inv_spread = lax.rsqrt(variance + EPSILON)
    normed = (centered * inv_spread[None, :, None]).reshape(pixels, channels)
    scaled = normed * norm_gain[None, :]
    first_act = jax.nn.silu(scaled).astype(jnp.bfloat16).reshape(tile_rows, tile_cols, channels)
    padded_first = with_rim(first_act)
    hidden_pre = apply_taps(padded_first, first_weight, tile_rows, tile_cols, False)
    second_act = (
        jax.nn.silu(hidden_pre).astype(jnp.bfloat16).reshape(tile_rows, tile_cols, channels)
    )
    padded_second = with_rim(second_act)
    features = (
        lifted + apply_taps(padded_second, second_weight, tile_rows, tile_cols, False)
    ).astype(jnp.bfloat16)
    features = features.reshape(tile_rows, tile_cols, channels)
    flat_cot = cotangent.reshape(pixels, channels)
    grad_act_two = apply_taps(with_rim(cotangent), second_weight, tile_rows, tile_cols, True)
    grad_hidden = (grad_act_two * silu_slope(hidden_pre)).astype(jnp.bfloat16)
    second_term = tap_grads(padded_second, flat_cot, tile_rows, tile_cols) * report
    grad_second = lax.psum(second_term, ("row", "col"))
    grad_act_one = apply_taps(
        with_rim(grad_hidden.reshape(tile_rows, tile_cols, channels)),
        first_weight,
        tile_rows,
        tile_cols,
        True,
    )
    first_term = tap_grads(padded_first, grad_hidden, tile_rows, tile_cols) * report
    grad_first = lax.psum(first_term, ("row", "col"))
    grad_scaled = grad_act_one * silu_slope(scaled)
    grad_normed = (grad_scaled * norm_gain[None, :]).reshape(pixels, GROUPS, per_group)
    normed_groups = normed.reshape(pixels, GROUPS, per_group)
    gain_term = jnp.sum(grad_scaled * normed, axis=0) * report
    grad_gain, plain_sum, cross_sum = lax.psum(
        (
            gain_term,
            jnp.sum(grad_normed, axis=(0, 2)),
            jnp.sum(grad_normed * normed_groups, axis=(0, 2)),
        ),
        ("row", "col"),
    )
    grad_lifted = (
        inv_spread[None, :, None]
        * (
            grad_normed
            - plain_sum[None, :, None] / members
            - normed_groups * cross_sum[None, :, None] / members
        )
    ).reshape(pixels, channels) + flat_cot.astype(jnp.float32)
    grad_lifted_low = grad_lifted.astype(jnp.bfloat16)
    land_term = jnp.sum(land_float[:, None] * grad_lifted, axis=0) * report
    lift_term = (
        jnp.einsum("hp,pd->hd", fine_input, grad_lifted_low, preferred_element_type=jnp.float32)
        * report
    )
    grad_lift, grad_land = lax.psum((lift_term, land_term), ("row", "col"))
    grad_fine = jnp.einsum(
        "hd,pd->hp", lift_weight, grad_lifted_low, preferred_element_type=jnp.float32
    )
    grad_fine = grad_fine.reshape(in_channels, 2, half_rows, tile_cols)
    grad_sums = jnp.einsum(
        "ia,hqij,jb->qhab", row_up, grad_fine, col_up, precision=PRECISE
    ).reshape(2, block_width)
    grad_slots = jnp.einsum("qs,qx->sx", selector, grad_sums, precision=PRECISE)
    grad_slots = grad_slots.reshape(3, 3, blocks_here, in_channels, coarse_rows * coarse_cols)
    returned = grad_slots[1, 1]
    for slot_row in range(3):
        for slot_col in range(3):
            if slot_row == 1 and slot_col == 1:
                continue
            portion = grad_slots[slot_row, slot_col]
            if slot_col != 1:
                portion = shifted(portion, "col", slot_col - 1)
            if slot_row != 1:
                portion = shifted(portion, "row", slot_row - 1)
            returned = returned + portion
    grad_coarse = returned[None, None]
    return (features, grad_coarse, grad_first, grad_second, grad_lift, grad_land, grad_gain)


def solution(mesh):
    in_specs = (
        P("row", "col", None, None, None),
        P("row", "col", None),
        P("row", "col", None),
        P("row", "col"),
        P(),
        P(),
        P(),
        P(),
        P(),
        P("row", "col", None),
    )
    out_specs = (P("row", "col", None), P("row", "col", None, None, None), P(), P(), P(), P(), P())
    return jax.shard_map(shards, mesh=mesh, in_specs=in_specs, out_specs=out_specs, check_vma=False)
```

profile of v0, /device:TPU:1, one launch (start us, length us, event | category | flops | bytes accessed | tf_op | source)
XLA Modules:
  0.0 932.1 jit_solution(5748169114810131329)
XLA Ops:
  7.2 4.7 collective-permute-start
  12.0 5.5 collective-permute-start.1
  20.1 2.4 collective-permute-start.13
  26.8 4.0 collective-permute-start.15
  32.8 1.9 collective-permute-start.2
  37.1 2.2 collective-permute-done.3
  45.3 117.3 %psum.63 = f32[32]{0:T(128)S(1)} all-reduce(f32[32]{0:T(128)S(1)} %reduce_sum.67), channel_id=1, replica_groups=mesh['row'=16,'col'=32] {'row','col'}, use_global_device_ids=true, to_apply=%region_2.3 | all-reduce | flops 32 | bytes 256 | tf_op jit(solution)/shard_map/psum | solution.py:148
  164.2 99.4 %psum.64 = f32[32]{0:T(128)S(1)} all-reduce(f32[32]{0:T(128)S(1)} %reduce_sum.73), channel_id=1, replica_groups=mesh['row'=16,'col'=32] {'row','col'}, use_global_device_ids=true, to_apply=%region_5.6 | all-reduce | flops 32 | bytes 256 | tf_op jit(solution)/shard_map/psum | solution.py:151
  264.5 3.3 collective-permute-start.4
  267.8 1.9 collective-permute-start.5
  270.0 2.8 collective-permute-done.5
  272.8 3.7 collective-permute-start.6
  278.2 2.9 collective-permute-done.7
  285.0 3.4 collective-permute-start.16
  288.3 1.9 collective-permute-start.17
  290.3 3.6 collective-permute-start.8
  293.9 2.1 collective-permute-start.9
  300.8 4.0 collective-permute-start.19
  304.8 1.9 collective-permute-start.10
  314.7 117.7 %all-reduce.1 = (f32[32]{0:T(128)S(1)}, f32[32]{0:T(128)S(1)}) all-reduce(f32[32]{0:T(128)S(1)} %reduce_sum.93, f32[32]{0:T(128)S(1)} %reduce_sum.90), channel_id=1, replica_groups=mesh['row'=16,'col'=32] {'row','col'}, use_global_device_ids=true, to_apply=%region_11.12 | all-reduce | flops 64 | bytes 512 | tf_op jit(solution)/shard_map/psum | solution.py:184
  443.6 4.9 collective-permute-start.23
  449.8 4.6 collective-permute-start.30
  459.5 3.6 collective-permute-start.22
  464.4 4.0 collective-permute-start.26
  468.5 2.5 collective-permute-start.29
  471.0 1.9 collective-permute-start.21
  473.0 1.9 collective-permute-start.24
  474.9 3.6 collective-permute-start.28
  478.6 2.4 collective-permute-start.31
  481.0 112.6 %all-reduce = (f32[20,128]{1,0:T(8,128)}, f32[128]{0:T(128)}, f32[128]{0:T(128)}) all-reduce(f32[20,128]{1,0:T(8,128)S(1)} %convolution_multiply_fusion, f32[128]{0:T(128)S(1)} %broadcast_multiply_fusion.3, f32[128]{0:T(128)S(1)} %broadcast_multiply_fusion.2), channel_id=1, replica_groups=mesh['row'=16,'col'=32] {'row','col'}, use_global_device_ids=true, to_apply=%region_14.15 | all-reduce | flops 2816 | bytes 22528 | tf_op jit(solution)/shard_map/psum | solution.py:206
  594.3 328.2 %all-reduce.5.cloned.1.call-done = (f32[9,128,128]{2,1,0:T(8,128)}, f32[9,128,128]{2,1,0:T(8,128)}) async-done(((f32[9,128,128]{2,1,0:T(8,128)}, f32[9,128,128]{2,1,0:T(8,128)}), (f32[9,128,128]{2,1,0:T(8,128)}, f32[9,128,128]{2,1,0:T(8,128)})) %all-reduce.5.cloned.1.call-update) | async-done | bytes 1179664 | tf_op jit(solution)/shard_map/psum | solution.py:179
  922.4 2.0 copy.276
  (222 shorter events, 57.8 us)
Async XLA Ops:
  7.2 915.3 %all-reduce.5.cloned.1.call-start = ((), (), s32[]{:S(2)}) async-start(), calls=%async_computation | async-start | bytes 2359296 | tf_op jit(solution)/shard_map/psum | solution.py:179
  7.2 24.8 %collective-permute-start = (bf16[1,1,2,20,128]{4,2,3,1,0:T(2,128)(2,1)}, bf16[1,1,2,20,128]{4,2,3,1,0:T(2,128)(2,1)S(1)}, u32[]{:S(2)}, u32[]{:S(2)}) collective-permute-start(bf16[1,1,2,20,128]{4,2,3,1,0:T(2,128)(2,1)} %param.10), channel_id=1, source_target_pairs={{0,32},{32,64},{64,96},{96,128},{128,160},{160,192},{192,224},{224... | collective-permute-start | bytes 30728 | tf_op jit(solution)/shard_map/ppermute | solution.py:22
  12.0 20.8 %collective-permute-start.1 = (bf16[1,1,2,20,128]{4,2,3,1,0:T(2,128)(2,1)}, bf16[1,1,2,20,128]{4,2,3,1,0:T(2,128)(2,1)S(1)}, u32[]{:S(2)}, u32[]{:S(2)}) collective-permute-start(bf16[1,1,2,20,128]{4,2,3,1,0:T(2,128)(2,1)} %param.10), channel_id=1, source_target_pairs={{32,0},{64,32},{96,64},{128,96},{160,128},{192,160},{224,192},{256... | collective-permute-start | bytes 30728 | tf_op jit(solution)/shard_map/ppermute | solution.py:23
  18.2 7.0 collective-permute-start.12
  20.1 5.1 collective-permute-start.13
  25.5 10.5 %collective-permute-start.14 = (bf16[34,1,128]{2,1,0:T(2,128)(2,1)S(1)}, bf16[34,1,128]{2,1,0:T(2,128)(2,1)S(1)}, u32[]{:S(2)}, u32[]{:S(2)}) collective-permute-start(bf16[34,1,128]{2,1,0:T(2,128)(2,1)S(1)} %get-tuple-element.113), channel_id=1, source_target_pairs={{1,0},{2,1},{3,2},{4,3},{5,4},{6,5},{7,6},{8,7},{9,8},{10,9},{11,1... | collective-permute-start | bytes 26120 | tf_op jit(solution)/shard_map/ppermute | solution.py:23
  26.8 9.2 collective-permute-start.15
  34.7 4.6 collective-permute-start.3
  264.5 5.4 collective-permute-start.4
  267.8 5.0 collective-permute-start.5
  272.8 5.4 collective-permute-start.6
  276.5 4.6 collective-permute-start.7
  285.0 14.2 %collective-permute-start.16 = (bf16[1,32,128]{2,1,0:T(8,128)(2,1)S(1)}, bf16[1,32,128]{2,1,0:T(8,128)(2,1)S(1)}, u32[]{:S(2)}, u32[]{:S(2)}) collective-permute-start(bf16[1,32,128]{2,1,0:T(8,128)(2,1)S(1)} %get-tuple-element.125), channel_id=1, source_target_pairs={{0,32},{32,64},{64,96},{96,128},{128,160},{160,192},{192,224},{224... | collective-permute-start | bytes 24584 | tf_op jit(solution)/shard_map/ppermute | solution.py:22
  288.3 10.8 %collective-permute-start.17 = (bf16[1,32,128]{2,1,0:T(8,128)(2,1)S(1)}, bf16[1,32,128]{2,1,0:T(8,128)(2,1)S(1)}, u32[]{:S(2)}, u32[]{:S(2)}) collective-permute-start(bf16[1,32,128]{2,1,0:T(8,128)(2,1)S(1)} %get-tuple-element.126), channel_id=1, source_target_pairs={{32,0},{64,32},{96,64},{128,96},{160,128},{192,160},{224,192},{256... | collective-permute-start | bytes 24584 | tf_op jit(solution)/shard_map/ppermute | solution.py:23
  290.3 14.5 %collective-permute-start.8 = (bf16[1,32,128]{2,1,0:T(8,128)(2,1)S(1)}, bf16[1,32,128]{2,1,0:T(8,128)(2,1)S(1)}, u32[]{:S(2)}, u32[]{:S(2)}) collective-permute-start(bf16[1,32,128]{2,1,0:T(8,128)(2,1)S(1)} %get-tuple-element.134), channel_id=1, source_target_pairs={{0,32},{32,64},{64,96},{96,128},{128,160},{160,192},{192,224},{224... | collective-permute-start | bytes 24584 | tf_op jit(solution)/shard_map/ppermute | solution.py:22
  293.9 10.8 %collective-permute-start.9 = (bf16[1,32,128]{2,1,0:T(8,128)(2,1)S(1)}, bf16[1,32,128]{2,1,0:T(8,128)(2,1)S(1)}, u32[]{:S(2)}, u32[]{:S(2)}) collective-permute-start(bf16[1,32,128]{2,1,0:T(8,128)(2,1)S(1)} %get-tuple-element.135), channel_id=1, source_target_pairs={{32,0},{64,32},{96,64},{128,96},{160,128},{192,160},{224,192},{256... | collective-permute-start | bytes 24584 | tf_op jit(solution)/shard_map/ppermute | solution.py:23
  299.5 8.8 collective-permute-start.18
  300.8 7.6 collective-permute-start.19
  304.8 7.8 collective-permute-start.10
  306.7 5.9 collective-permute-start.11
  441.7 21.4 %collective-permute-start.20 = (f32[2,20,128]{2,0,1:T(2,128)}, f32[2,20,128]{2,0,1:T(2,128)}, u32[]{:S(2)}, u32[]{:S(2)}) collective-permute-start(f32[2,20,128]{2,0,1:T(2,128)} %bitcast.403), channel_id=1, source_target_pairs={{1,0},{2,1},{3,2},{4,3},{5,4},{6,5},{7,6},{8,7},{9,8},{10,9},{11,1... | collective-permute-start | bytes 61448 | tf_op jit(solution)/shard_map/ppermute | solution.py:31
  443.6 20.8 %collective-permute-start.23 = (f32[2,20,128]{2,0,1:T(2,128)}, f32[2,20,128]{2,0,1:T(2,128)}, u32[]{:S(2)}, u32[]{:S(2)}) collective-permute-start(f32[2,20,128]{2,0,1:T(2,128)} %bitcast.401), channel_id=1, source_target_pairs={{0,1},{1,2},{2,3},{3,4},{4,5},{5,6},{6,7},{7,8},{8,9},{9,10},{10,1... | collective-permute-start | bytes 61448 | tf_op jit(solution)/shard_map/ppermute | solution.py:31
  448.5 19.9 %collective-permute-start.27 = (f32[2,20,128]{2,0,1:T(2,128)S(1)}, f32[2,20,128]{2,0,1:T(2,128)}, u32[]{:S(2)}, u32[]{:S(2)}) collective-permute-start(f32[2,20,128]{2,0,1:T(2,128)S(1)} %bitcast.463), channel_id=1, source_target_pairs={{1,0},{2,1},{3,2},{4,3},{5,4},{6,5},{7,6},{8,7},{9,8},{10,9},{11,1... | collective-permute-start | bytes 61448 | tf_op jit(solution)/shard_map/ppermute | solution.py:31
  449.8 21.2 %collective-permute-start.30 = (f32[2,20,128]{2,0,1:T(2,128)S(1)}, f32[2,20,128]{2,0,1:T(2,128)}, u32[]{:S(2)}, u32[]{:S(2)}) collective-permute-start(f32[2,20,128]{2,0,1:T(2,128)S(1)} %bitcast.462), channel_id=1, source_target_pairs={{0,1},{1,2},{2,3},{3,4},{4,5},{5,6},{6,7},{7,8},{8,9},{9,10},{10,1... | collective-permute-start | bytes 61448 | tf_op jit(solution)/shard_map/ppermute | solution.py:31
  459.5 13.5 %collective-permute-start.22 = (f32[2,20,128]{2,0,1:T(2,128)S(1)}, f32[2,20,128]{2,0,1:T(2,128)S(1)}, u32[]{:S(2)}, u32[]{:S(2)}) collective-permute-start(f32[2,20,128]{2,0,1:T(2,128)S(1)} %bitcast.467), channel_id=1, source_target_pairs={{32,0},{64,32},{96,64},{128,96},{160,128},{192,160},{224,192},{256... | collective-permute-start | bytes 61448 | tf_op jit(solution)/shard_map/ppermute | solution.py:31
  463.1 11.8 %collective-permute-start.25 = (f32[2,20,128]{2,0,1:T(2,128)S(1)}, f32[2,20,128]{2,0,1:T(2,128)S(1)}, u32[]{:S(2)}, u32[]{:S(2)}) collective-permute-start(f32[2,20,128]{2,0,1:T(2,128)S(1)} %bitcast.466), channel_id=1, source_target_pairs={{1,0},{2,1},{3,2},{4,3},{5,4},{6,5},{7,6},{8,7},{9,8},{10,9},{11,1... | collective-permute-start | bytes 61448 | tf_op jit(solution)/shard_map/ppermute | solution.py:31
  464.4 14.1 %collective-permute-start.26 = (f32[2,20,128]{2,0,1:T(2,128)S(1)}, f32[2,20,128]{2,0,1:T(2,128)S(1)}, u32[]{:S(2)}, u32[]{:S(2)}) collective-permute-start(f32[2,20,128]{2,0,1:T(2,128)S(1)} %bitcast.464), channel_id=1, source_target_pairs={{0,1},{1,2},{2,3},{3,4},{4,5},{5,6},{6,7},{7,8},{8,9},{9,10},{10,1... | collective-permute-start | bytes 61448 | tf_op jit(solution)/shard_map/ppermute | solution.py:31
  468.5 125.1 %collective-permute-start.29 = (f32[2,20,128]{2,0,1:T(2,128)S(1)}, f32[2,20,128]{2,0,1:T(2,128)S(1)}, u32[]{:S(2)}, u32[]{:S(2)}) collective-permute-start(f32[2,20,128]{2,0,1:T(2,128)S(1)} %bitcast.465), channel_id=1, source_target_pairs={{0,32},{32,64},{64,96},{96,128},{128,160},{160,192},{192,224},{224... | collective-permute-start | bytes 61448 | tf_op jit(solution)/shard_map/ppermute | solution.py:31
  471.0 122.6 %collective-permute-start.21 = (f32[2,20,128]{2,0,1:T(2,128)}, f32[2,20,128]{2,0,1:T(2,128)S(1)}, u32[]{:S(2)}, u32[]{:S(2)}) collective-permute-start(f32[2,20,128]{2,0,1:T(2,128)} %collective-permute-done.20), channel_id=1, source_target_pairs={{32,0},{64,32},{96,64},{128,96},{160,128},{192,160},{224,192},{256... | collective-permute-start | bytes 61448 | tf_op jit(solution)/shard_map/ppermute | solution.py:31
  473.0 120.6 %collective-permute-start.24 = (f32[2,20,128]{2,0,1:T(2,128)}, f32[2,20,128]{2,0,1:T(2,128)S(1)}, u32[]{:S(2)}, u32[]{:S(2)}) collective-permute-start(f32[2,20,128]{2,0,1:T(2,128)} %collective-permute-done.23), channel_id=1, source_target_pairs={{32,0},{64,32},{96,64},{128,96},{160,128},{192,160},{224,192},{256... | collective-permute-start | bytes 61448 | tf_op jit(solution)/shard_map/ppermute | solution.py:31
  474.9 118.7 %collective-permute-start.28 = (f32[2,20,128]{2,0,1:T(2,128)}, f32[2,20,128]{2,0,1:T(2,128)S(1)}, u32[]{:S(2)}, u32[]{:S(2)}) collective-permute-start(f32[2,20,128]{2,0,1:T(2,128)} %collective-permute-done.27), channel_id=1, source_target_pairs={{0,32},{32,64},{64,96},{96,128},{128,160},{160,192},{192,224},{224... | collective-permute-start | bytes 61448 | tf_op jit(solution)/shard_map/ppermute | solution.py:31
  478.6 115.0 %collective-permute-start.31 = (f32[2,20,128]{2,0,1:T(2,128)}, f32[2,20,128]{2,0,1:T(2,128)S(1)}, u32[]{:S(2)}, u32[]{:S(2)}) collective-permute-start(f32[2,20,128]{2,0,1:T(2,128)} %collective-permute-done.30), channel_id=1, source_target_pairs={{0,32},{32,64},{64,96},{96,128},{128,160},{160,192},{192,224},{224... | collective-permute-start | bytes 61448 | tf_op jit(solution)/shard_map/ppermute | solution.py:31
  (17 other events, 102.5 us)
Sparse Core Ops, SparseCore 0:
  457.1 465.2 all-reduce.4
where the time goes:
time: 935 us; the launch traced here: 932 us
  blocking collectives  447 us (48%)
  waiting for transfers between devices  336 us (36%)
  starting transfers between devices  86.2 us (9%)
  matrix products  23.4 us (3%)
  local copies, waits for them, and re-layouts  16.5 us (2%)
  between operations  15.3 us (2%)
    psum x1, waiting for transfers between devices, shards(): grad_first = lax.psum(first_term, ('row', 'col'))  328 us
    psum x1, blocking collectives, shards(): lax.psum((gain_term, jnp.sum(grad_normed, axis=(0, 2)), jnp.sum(grad_norm...  118 us
    psum x1, blocking collectives, shards(): group_total = lax.psum(jnp.sum(grouped, axis=(0, 2)), ('row', 'col'))  117 us
    psum x1, blocking collectives, shards(): grad_lift, grad_land = lax.psum((lift_term, land_term), ('row', 'col'))  113 us
    psum x1, blocking collectives, shards(): lax.psum(jnp.sum(centered * centered, axis=(0, 2)), ('row', 'col'))  99.4 us
    ppermute x12, starting transfers between devices, shifted(): return lax.ppermute(x, axis, pairs)  33.3 us
    ppermute x10, starting transfers between devices, extended(): before = lax.ppermute(last, axis, up)  32.4 us
    ppermute x10, starting transfers between devices, extended(): after = lax.ppermute(leading, axis, down)  20.4 us
  transfers between devices with their start and end apart: 33, of which 4 were waited for; matrix products, arithmetic and copies ran while one was open for 2% of the time, Pallas kernels for 0%

commit v1 on v0

v1 whole, which is shorter than its diff:
```python
import math

import jax
import jax.numpy as jnp
from jax import lax
from jax.experimental import pallas as pl
from jax.experimental.pallas import tpu as pltpu
from jax.sharding import PartitionSpec as P

GROUPS = 32
EPSILON = 1e-05
MESH = pl.DeviceIdType.MESH
F32 = jnp.float32
BF16 = jnp.bfloat16

TILE = 32
ROWS = TILE + 4
WIDE = 48
LEFT = 8
CH = 128
CIN = 20
PIX = TILE * TILE
TAPS = 9
HALF = TAPS * CH


def log2(n):
    return n.bit_length() - 1


def size_of(group):
    n = 1
    for _, _, count in group:
        n *= count
    return n


def place_in(group, at):
    m = 0
    for axis, stride, count in group:
        m = (m << log2(count)) | ((at[axis] >> log2(stride)) & (count - 1))
    return m


def member_of(group, at, m):
    new = dict(at)
    for axis, stride, count in reversed(group):
        digit = m & (count - 1)
        m = m >> log2(count)
        new[axis] = (new[axis] & ~((count - 1) * stride)) | (digit << log2(stride))
    return (new["row"], new["col"])


def each_other(group, at, act):
    n = size_of(group)
    me = place_in(group, at)

    def body(k, carry):
        m = (me + k) & (n - 1)
        act(member_of(group, at, m), m)
        return carry

    lax.fori_loop(1, n, body, 0)


def remote(src, dst, send, recv, device):
    return pltpu.make_async_remote_copy(
        src_ref=src,
        dst_ref=dst,
        send_sem=send,
        recv_sem=recv,
        device_id=device,
        device_id_type=MESH,
    )


def dot(a, b):
    return jnp.dot(a, b, preferred_element_type=F32)


def dot_tn(a, b):
    return lax.dot_general(a, b, (((0,), (0,)), ((), ())), preferred_element_type=F32)


def dot_nt(a, b):
    return lax.dot_general(a, b, (((1,), (1,)), ((), ())), preferred_element_type=F32)


def split_two(x):
    hi = x.astype(BF16)
    return hi, (x - hi.astype(F32)).astype(BF16)


def split_three(x):
    hi = x.astype(BF16)
    rest = x - hi.astype(F32)
    mid = rest.astype(BF16)
    return hi, mid, (rest - mid.astype(F32)).astype(BF16)


def sigmoid(v):
    return 1.0 / (1.0 + jnp.exp(-v))


def group_sums(v):
    lane = lax.broadcasted_iota(jnp.int32, v.shape, 1)
    one = v + jnp.where((lane & 1) == 1, pltpu.roll(v, 1, 1), pltpu.roll(v, CH - 1, 1))
    return one + jnp.where((lane & 2) == 2, pltpu.roll(one, 2, 1), pltpu.roll(one, CH - 2, 1))


def kernel(
    n_row,
    n_col,
    coarse,
    ids,
    quad,
    land,
    lift_w,
    land_v,
    gain_ref,
    w1_hbm,
    w2_hbm,
    cot_hbm,
    feat,
    gcoarse,
    grads,
    glift,
    gland,
    ggain,
    padf,
    cand,
    up,
    ft,
    wext,
    w1,
    w2,
    cotv,
    wt1,
    wt2,
    ext,
    rh_s,
    rh_r,
    ch_s,
    ch_r,
    x3a,
    x3b,
    x3c,
    x3g,
    gic,
    gig,
    t2,
    gsc,
    glb,
    a1c,
    a1x,
    a1z,
    a2c,
    a2x,
    a2z,
    a3c,
    a3x,
    a3z,
    gbuf,
    cbuf,
    acc,
    xyb,
    zsrc,
    zb,
    ret_s,
    ret_r,
    dma,
    snd,
    rcv,
):
    row = lax.axis_index("row")
    col = lax.axis_index("col")
    at = {"row": row, "col": col}
    core_g = (("row", 1, 2),)
    xy_g = (("row", 2, n_row // 2), ("col", n_col // 2, 2))
    z_g = (("col", 1, n_col // 2),)
    n_xy = size_of(xy_g)
    n_z = size_of(z_g)
    members = float(n_row * TILE * n_col * TILE * (CH // GROUPS))
    report = 1.0 / math.sqrt(n_row * TILE * n_col * TILE)
    pixels_all = float(n_row * TILE * n_col * TILE)

    core = place_in(core_g, at)
    xy = place_in(xy_g, at)
    z = place_in(z_g, at)
    core_dev = member_of(core_g, at, 1 - core)

    def near(dr, dc):
        return ((row + dr + n_row) & (n_row - 1), (col + dc + n_col) & (n_col - 1))

    around = [(dr, dc) for dr in (-1, 0, 1) for dc in (-1, 0, 1)]

    def waiter(ref, k):
        return remote(ref, ref, snd.at[k], rcv.at[k], core_dev)

    loads = [
        pltpu.make_async_copy(w1_hbm, w1, dma.at[0]),
        pltpu.make_async_copy(w2_hbm, w2, dma.at[1]),
        pltpu.make_async_copy(cot_hbm, cotv, dma.at[2]),
    ]
    for load in loads:
        load.start()

    barrier = pltpu.get_barrier_semaphore()

    def greet(device, m):
        pl.semaphore_signal(barrier, inc=1, device_id=device, device_id_type=MESH)

    for dr, dc in around:
        if (dr, dc) != (0, 0):
            greet(near(dr, dc), 0)
    for group in (core_g, xy_g, z_g):
        each_other(group, at, greet)

    padf[...] = jnp.zeros_like(padf)
    padf[0:2, 0:CIN, :] = coarse[0, 0].astype(F32)
    padf[2, 0:CIN, :] = lift_w[...].astype(F32)
    cand[4] = padf[0:2].astype(BF16)

    codes = []
    for k in range(ids.shape[2]):
        block = ids[0, 0, k]
        owner = block >> 1
        slot_row = (owner >> log2(n_col)) - row + 1
        slot_col = (owner & (n_col - 1)) - col + 1
        codes.append(((quad[0, 0, k] * 9) + slot_row * 3 + slot_col) * 2 + (block & 1))

    def picks(q, s, m):
        want = (q * 9 + s) * 2 + m
        total = jnp.float32(0.0)
        for code in codes:
            total = total + jnp.where(code == want, jnp.float32(1.0), jnp.float32(0.0))
        return total

    weight = {(q, s, m): picks(q, s, m) for q in range(2) for s in range(9) for m in range(2)}

    pl.semaphore_wait(barrier, 8 + 1 + n_xy - 1 + n_z - 1)

    for s, (dr, dc) in enumerate(around):
        if s != 4:
            remote(cand.at[4], cand.at[8 - s], snd.at[0], rcv.at[0], near(dr, dc)).start()

    fine = lax.broadcasted_iota(jnp.int32, (CH, 512), 1)
    cell = lax.broadcasted_iota(jnp.int32, (CH, 512), 0)

    def hat(fine_at, cell_at, count):
        where = jnp.clip((fine_at.astype(F32) + 0.5) * 0.5 - 0.5, 0.0, count - 1.0)
        return jnp.maximum(1.0 - jnp.abs(where - cell_at.astype(F32)), 0.0)

    up[...] = (hat(fine >> 5, cell >> 4, 8) * hat(fine & 31, cell & 15, 16)).astype(BF16)

    pix = lax.broadcasted_iota(jnp.int32, (TILE, PIX), 1)
    line = lax.broadcasted_iota(jnp.int32, (TILE, PIX), 0)
    spread = jnp.where((pix & 31) == line, 1.0, 0.0).astype(BF16)
    lines = dot(land[...].astype(F32).astype(BF16), spread)
    lines = jnp.where((pix >> 5) == line, lines, 0.0).astype(BF16)
    wext[0:32] = padf[2].astype(BF16)
    for k, part in enumerate(split_three(jnp.broadcast_to(land_v[...], (32, CH)))):
        ft[32 * (k + 1) : 32 * (k + 2), :] = lines
        wext[32 * (k + 1) : 32 * (k + 2), :] = part

    for lo, hi in ((0, LEFT), (LEFT + TILE, WIDE)):
        ext[:, :, lo:hi, :] = jnp.zeros((2, ROWS, 8, CH), F32)
    for edge in (0, ROWS - 1):
        gic[edge] = jnp.zeros((WIDE, CH), BF16)
        gig[edge] = jnp.zeros((WIDE, CH), BF16)

    for load in loads:
        load.wait()
    for k in range(TAPS):
        wt1[:, k * CH : (k + 1) * CH] = w1[8 - k]
        wt2[:, k * CH : (k + 1) * CH] = w2[8 - k]
    ext[1, 2 : 2 + TILE, LEFT : LEFT + TILE, :] = cotv[...].astype(F32)

    waiter(cand.at[pl.ds(0, 8)], 0).wait_recv()
    sums = []
    for q in range(2):
        total = jnp.zeros((32, CH), F32)
        for s in range(9):
            for m in range(2):
                total = total + weight[q, s, m] * cand[s, m].astype(F32)
        sums.append(total)
    parts = split_three(jnp.concatenate(sums, axis=0))
    raised = dot(jnp.concatenate(parts, axis=0), up[...])
    raised = raised[0:64] + raised[64:128] + raised[128:192]
    ft[0:32, 0:512] = raised[0:32].astype(BF16)
    ft[0:32, 512:1024] = raised[32:64].astype(BF16)
    lifted = dot_tn(ft[...], wext[...])
    ext[0, 2 : 2 + TILE, LEFT : LEFT + TILE, :] = lifted.reshape(TILE, TILE, CH)
    mean_here = jnp.sum(lifted, axis=0, keepdims=True) * (1.0 / PIX)
    apart = lifted - mean_here
    square_here = jnp.sum(apart * apart, axis=0, keepdims=True)

    def start_level(group, buf, k, value):
        me = place_in(group, at)
        buf[me] = value

        def send(device, m):
            remote(buf.at[me], buf.at[me], snd.at[k], rcv.at[k], device).start()

        each_other(group, at, send)

    def end_level(buf, k):
        waiter(buf.at[pl.ds(0, buf.shape[0] - 1)], k).wait()
        return [buf[i] for i in range(buf.shape[0])]

    def add_up(values):
        while len(values) > 1:
            values = [a + b for a, b in zip(values[::2], values[1::2])]
        return values[0]

    def merge(values, count):
        mean = add_up([v[0:1] for v in values]) * (1.0 / len(values))
        square = add_up([v[1:2] for v in values])
        off = add_up([(v[0:1] - mean) * (v[0:1] - mean) for v in values])
        return jnp.concatenate([mean, square + count * off], axis=0)

    start_level(core_g, a1c, 1, jnp.concatenate([mean_here, square_here], axis=0))

    rh_s[0] = ext[:, 2:4, LEFT : LEFT + TILE, :]
    rh_s[1] = ext[:, TILE : TILE + 2, LEFT : LEFT + TILE, :]

    moments = merge(end_level(a1c, 1), float(PIX))
    start_level(xy_g, a1x, 2, moments)
    remote(rh_s.at[0], rh_r.at[0], snd.at[4], rcv.at[4], near(-1, 0)).start()
    remote(rh_s.at[1], rh_r.at[1], snd.at[4], rcv.at[4], near(1, 0)).start()

    moments = merge(end_level(a1x, 2), float(2 * PIX))
    start_level(z_g, a1z, 3, moments)

    waiter(rh_r, 4).wait()
    ext[:, 2 + TILE : 4 + TILE, LEFT : LEFT + TILE, :] = rh_r[0]
    ext[:, 0:2, LEFT : LEFT + TILE, :] = rh_r[1]
    for a in range(2):
        for k in range(2):
            ch_s[0, a, k, 0:ROWS, :] = ext[a, :, LEFT + k, :]
            ch_s[1, a, k, 0:ROWS, :] = ext[a, :, LEFT + TILE - 2 + k, :]
    remote(ch_s.at[0], ch_r.at[0], snd.at[5], rcv.at[5], near(0, -1)).start()
    remote(ch_s.at[1], ch_r.at[1], snd.at[5], rcv.at[5], near(0, 1)).start()
    waiter(ch_r, 5).wait()
    for a in range(2):
        for k in range(2):
            ext[a, :, LEFT + TILE + k, :] = ch_r[0, a, k, 0:ROWS, :]
            ext[a, :, LEFT - 2 + k, :] = ch_r[1, a, k, 0:ROWS, :]

    row_lo = jnp.where(row == 0, 2, 0)
    row_hi = jnp.where(row == n_row - 1, 2 + TILE, ROWS)
    col_lo = jnp.where(col == 0, LEFT, 0)
    col_hi = jnp.where(col == n_col - 1, LEFT + TILE, WIDE)

    def masks(first, count):
        r = lax.broadcasted_iota(jnp.int32, (count, WIDE, CH), 0) + first
        c = lax.broadcasted_iota(jnp.int32, (count, WIDE, CH), 1)
        in_grid = (r >= row_lo) & (r < row_hi) & (c >= col_lo) & (c < col_hi)
        in_tile = (r >= 2) & (r < 2 + TILE) & (c >= LEFT) & (c < LEFT + TILE)
        shape = (count * WIDE, CH)
        return in_grid.reshape(shape), in_tile.reshape(shape)

    def put_taps(x3, first, count, flat):
        length = count * WIDE
        x3[pl.ds(first, count), :, 0:CH] = pltpu.roll(flat, 1, 0).astype(BF16).reshape(count, WIDE, CH)
        x3[pl.ds(first, count), :, CH : 2 * CH] = flat.astype(BF16).reshape(count, WIDE, CH)
        x3[pl.ds(first, count), :, 2 * CH :] = (
            pltpu.roll(flat, length - 1, 0).astype(BF16).reshape(count, WIDE, CH)
        )

    def windows(x3, first, count):
        return jnp.concatenate(
            [x3[pl.ds(first - 1 + u, count)].reshape(count * WIDE, 3 * CH) for u in range(3)],
            axis=1,
        )

    def loop(trips, body):
        def step(i, carry):
            body(i)
            return carry

        lax.fori_loop(0, trips, step, 0)

    def cot_rows(i):
        first = i * 4
        in_grid, in_tile = masks(first, 4)
        flat = ext[1, pl.ds(first, 4)].reshape(4 * WIDE, CH)
        put_taps(x3c, first, 4, jnp.where(in_grid, flat, 0.0))
        gic[pl.ds(first, 4)] = jnp.where(in_tile, flat, 0.0).astype(BF16).reshape(4, WIDE, CH)

    loop(9, cot_rows)

    def cot_conv(i):
        first = 1 + i * 17
        t2[pl.ds(first, 17)] = dot_nt(windows(x3c, first, 17), wt2[...]).reshape(17, WIDE, CH)

    loop(2, cot_conv)

    moments = merge(end_level(a1z, 3), float(2 * n_xy * PIX))
    mean_ch = moments[0:1]
    group_mean = group_sums(mean_ch) * (GROUPS / CH)
    off = mean_ch - group_mean
    variance = group_sums(moments[1:2] + pixels_all * off * off) / members
    inv_spread = lax.rsqrt(variance + EPSILON)
    gain = gain_ref[...]

    def act_rows(i):
        first = i * 4
        in_grid, _ = masks(first, 4)
        flat = ext[0, pl.ds(first, 4)].reshape(4 * WIDE, CH)
        scaled = (flat - group_mean) * inv_spread * gain
        act = scaled * sigmoid(scaled)
        put_taps(x3a, first, 4, jnp.where(in_grid, act, 0.0))

    loop(9, act_rows)

    def hidden_rows(i):
        first = 1 + i * 17
        in_grid, in_tile = masks(first, 17)
        hidden = dot(windows(x3a, first, 17), w1[...].reshape(HALF, CH))
        gate = sigmoid(hidden)
        act = jnp.where(in_grid, hidden * gate, 0.0)
        slope = gate * (1.0 + hidden * (1.0 - gate))
        grad = jnp.where(in_grid, t2[pl.ds(first, 17)].reshape(17 * WIDE, CH) * slope, 0.0)
        put_taps(x3b, first, 17, act)
        put_taps(x3g, first, 17, grad)
        gig[pl.ds(first, 17)] = jnp.where(in_tile, grad, 0.0).astype(BF16).reshape(17, WIDE, CH)

    loop(2, hidden_rows)

    def tap_grads(x3, gi, half):
        length = (ROWS - 2) * WIDE
        grad = jnp.concatenate(
            [gi[2 - u : 2 - u + ROWS - 2].reshape(length, CH) for u in range(3)], axis=1
        )
        out = dot_tn(x3[1 : ROWS - 1].reshape(length, 3 * CH), grad)
        for u in range(3):
            for v in range(3):
                gbuf[half, (3 * u + v) * CH : (3 * u + v + 1) * CH, :] = out[
                    v * CH : (v + 1) * CH, u * CH : (u + 1) * CH
                ]

    tap_grads(x3b, gic, 0)
    tap_grads(x3a, gig, 1)

    swap = remote(gbuf.at[1 - core], cbuf, snd.at[6], rcv.at[6], core_dev)
    swap.start()

    def back_rows(i, sums):
        first = 2 + i * 8
        inner = slice(LEFT, LEFT + TILE)
        grad_act = dot_nt(windows(x3g, first, 8), wt1[...]).reshape(8, WIDE, CH)[:, inner, :]
        normed = (ext[0, pl.ds(first, 8), inner, :] - group_mean[None]) * inv_spread[None]
        scaled = normed * gain[None]
        gate = sigmoid(scaled)
        grad = grad_act * (gate * (1.0 + scaled * (1.0 - gate)))
        gsc[pl.ds(i * 8, 8)] = grad
        plain, cross = sums
        return (
            plain + jnp.sum(grad.reshape(32, 8, CH), axis=0),
            cross + jnp.sum((grad * normed).reshape(32, 8, CH), axis=0),
        )

    nothing = jnp.zeros((8, CH), F32)
    plain, cross = lax.fori_loop(0, 4, back_rows, (nothing, nothing))
    both = jnp.concatenate(
        [jnp.sum(plain, axis=0, keepdims=True), jnp.sum(cross, axis=0, keepdims=True)], axis=0
    )
    start_level(core_g, a2c, 7, both)

    swap.wait_recv()
    acc[...] = gbuf[core] + cbuf[...]
    share = HALF // n_xy

    def share_of(ref, m):
        return ref.at[pl.ds(pl.multiple_of(m * share, 8), share)]

    def send_share(device, m):
        remote(share_of(acc, m), xyb.at[xy], snd.at[8], rcv.at[8], device).start()

    start_level(xy_g, a2x, 9, add_up(end_level(a2c, 7)))
    each_other(xy_g, at, send_share)
    xyb[xy] = acc[pl.ds(pl.multiple_of(xy * share, 8), share), :]

    def out_rows(i):
        first = 2 + i * 16
        inner = slice(LEFT, LEFT + TILE)
        out = dot(windows(x3b, first, 16), w2[...].reshape(HALF, CH)).reshape(16, WIDE, CH)
        feat[pl.ds(i * 16, 16)] = (ext[0, pl.ds(first, 16), inner, :] + out[:, inner, :]).astype(BF16)

    loop(2, out_rows)

    start_level(z_g, a2z, 10, add_up(end_level(a2x, 9)))

    waiter(xyb.at[pl.ds(0, n_xy - 1)], 8).wait()
    zsrc[...] = add_up([xyb[i] for i in range(n_xy)])
    tiles = share // 8
    turn = (xy + 8 * core) & (n_z - 1)
    mine = (z - turn) & (n_z - 1)
    owner = mine < tiles
    strip = pl.ds(pl.multiple_of(jnp.minimum(mine, tiles - 1) * 8, 8), 8)

    def send_tile(t, carry):
        goal = (t + turn) & (n_z - 1)

        @pl.when(goal != z)
        def _():
            remote(
                zsrc.at[pl.ds(pl.multiple_of(t * 8, 8), 8)],
                zb.at[z],
                snd.at[11],
                rcv.at[11],
                member_of(z_g, at, goal),
            ).start()

        return carry

    lax.fori_loop(0, tiles, send_tile, 0)

    totals = add_up(end_level(a2z, 10))
    ggain[...] = totals[1:2] * report
    plain_sum = group_sums(totals[0:1] * gain) * (1.0 / members)
    cross_sum = group_sums(totals[1:2] * gain) * (1.0 / members)

    def lifted_rows(i):
        first = 2 + i * 8
        inner = slice(LEFT, LEFT + TILE)
        normed = (ext[0, pl.ds(first, 8), inner, :] - group_mean[None]) * inv_spread[None]
        grad = gsc[pl.ds(i * 8, 8)] * gain[None] - plain_sum[None] - normed * cross_sum[None]
        grad = inv_spread[None] * grad + ext[1, pl.ds(first, 8), inner, :]
        hi, lo = split_two(grad.reshape(256, CH))
        spot = pl.ds(pl.multiple_of(i * 256, 256), 256)
        glb[spot, 0:CH] = hi
        glb[spot, CH:] = lo

    loop(4, lifted_rows)
    both = dot(ft[...], glb[...])
    on_land = jnp.sum(both[32:64, 0:CH] + both[32:64, CH:], axis=0, keepdims=True)
    which = lax.broadcasted_iota(jnp.int32, (24, CH), 0)
    start_level(core_g, a3c, 12, jnp.where(which == CIN, on_land, both[0:24, 0:CH]))

    fine_hi, fine_lo = split_two(dot_nt(wext[0:32], glb[:, 0:CH]))
    stacked = jnp.concatenate(
        [fine_hi[:, 0:512], fine_hi[:, 512:], fine_lo[:, 0:512], fine_lo[:, 512:]], axis=0
    )
    lowered = dot_nt(stacked, up[...])
    lowered = lowered[0:64] + lowered[64:128]
    for s, (dr, dc) in enumerate(around):
        for m in range(2):
            ret_s[s, m] = weight[0, s, m] * lowered[0:24] + weight[1, s, m] * lowered[32:56]

    start_level(xy_g, a3x, 13, add_up(end_level(a3c, 12)))
    for s, (dr, dc) in enumerate(around):
        if s != 4:
            remote(ret_s.at[s], ret_r.at[8 - s], snd.at[14], rcv.at[14], near(dr, dc)).start()

    @pl.when(owner)
    def _():
        zb[z] = zsrc[strip, :]
        waiter(zb.at[pl.ds(0, n_z - 1)], 11).wait_recv()
        waiter(zsrc.at[pl.ds(0, share - 8)], 11).wait_send()
        whole = add_up([zb[i] for i in range(n_z)]) * report
        spot = pl.ds(pl.multiple_of(xy * share + mine * 8, 8), 8)
        grads[core, spot, :] = whole

        def send_whole(device, m):
            piece = grads.at[core, spot]
            remote(piece, piece, snd.at[15], rcv.at[15], device).start()

        each_other(z_g, at, send_whole)

    @pl.when(jnp.logical_not(owner))
    def _():
        waiter(zsrc, 11).wait_send()

    start_level(z_g, a3z, 16, add_up(end_level(a3x, 13)))

    @pl.when(owner)
    def _():
        waiter(zb.at[pl.ds(0, n_z - 1)], 15).wait_send()
        waiter(zsrc.at[pl.ds(0, share - 8)], 15).wait_recv()

    @pl.when(jnp.logical_not(owner))
    def _():
        waiter(zsrc, 15).wait_recv()

    here = grads.at[core, pl.ds(pl.multiple_of(xy * share, 8), share)]

    def send_back(device, m):
        remote(here, here, snd.at[17], rcv.at[17], device).start()

    each_other(xy_g, at, send_back)

    waiter(ret_r.at[pl.ds(0, 8)], 14).wait()
    for m in range(2):
        total = ret_s[4, m]
        for s in range(9):
            if s != 4:
                total = total + ret_r[s, m]
        gcoarse[0, 0, m] = total[0:CIN]

    totals = add_up(end_level(a3z, 16)) * report
    glift[...] = totals[0:CIN]
    gland[...] = totals[CIN : CIN + 1]

    waiter(xyb.at[pl.ds(0, n_xy - 1)], 17).wait()
    half = remote(grads.at[core], grads.at[core], snd.at[18], rcv.at[18], core_dev)
    half.start()
    waiter(cand.at[pl.ds(0, 8)], 0).wait_send()
    swap.wait_send()
    half.wait()


def shards(*args):
    (
        coarse_blocks,
        block_ids,
        quadrant,
        land_mask,
        lift_weight,
        land_vector,
        norm_gain,
        first_weight,
        second_weight,
        cotangent,
    ) = args
    n_row, n_col = lax.axis_size("row"), lax.axis_size("col")
    n_xy, n_z = n_row, n_col // 2

    def body(*refs):
        kernel(n_row, n_col, *refs)

    vmem = pl.BlockSpec(memory_space=pltpu.VMEM)
    smem = pl.BlockSpec(memory_space=pltpu.SMEM)
    anywhere = pl.BlockSpec(memory_space=pl.ANY)
    scratch = [
        pltpu.VMEM((3, 32, CH), F32),
        pltpu.VMEM((9, 2, 32, CH), BF16),
        pltpu.VMEM((CH, 512), BF16),
        pltpu.VMEM((CH, PIX), BF16),
        pltpu.VMEM((CH, CH), BF16),
        pltpu.VMEM((TAPS, CH, CH), BF16),
        pltpu.VMEM((TAPS, CH, CH), BF16),
        pltpu.VMEM((TILE, TILE, CH), BF16),
        pltpu.VMEM((CH, HALF), BF16),
        pltpu.VMEM((CH, HALF), BF16),
        pltpu.VMEM((2, ROWS, WIDE, CH), F32),
        pltpu.VMEM((2, 2, 2, TILE, CH), F32),
        pltpu.VMEM((2, 2, 2, TILE, CH), F32),
        pltpu.VMEM((2, 2, 2, 40, CH), F32),
        pltpu.VMEM((2, 2, 2, 40, CH), F32),
        pltpu.VMEM((ROWS, WIDE, 3 * CH), BF16),
        pltpu.VMEM((ROWS, WIDE, 3 * CH), BF16),
        pltpu.VMEM((ROWS, WIDE, 3 * CH), BF16),
        pltpu.VMEM((ROWS, WIDE, 3 * CH), BF16),
        pltpu.VMEM((ROWS, WIDE, CH), BF16),
        pltpu.VMEM((ROWS, WIDE, CH), BF16),
        pltpu.VMEM((ROWS, WIDE, CH), F32),
        pltpu.VMEM((TILE, TILE, CH), F32),
        pltpu.VMEM((PIX, 2 * CH), BF16),
        pltpu.VMEM((2, 2, CH), F32),
        pltpu.VMEM((n_xy, 2, CH), F32),
        pltpu.VMEM((n_z, 2, CH), F32),
        pltpu.VMEM((2, 2, CH), F32),
        pltpu.VMEM((n_xy, 2, CH), F32),
        pltpu.VMEM((n_z, 2, CH), F32),
        pltpu.VMEM((2, 24, CH), F32),
        pltpu.VMEM((n_xy, 24, CH), F32),
        pltpu.VMEM((n_z, 24, CH), F32),
        pltpu.VMEM((2, HALF, CH), F32),
        pltpu.VMEM((HALF, CH), F32),
        pltpu.VMEM((HALF, CH), F32),
        pltpu.VMEM((n_xy, HALF // n_xy, CH), F32),
        pltpu.VMEM((HALF // n_xy, CH), F32),
        pltpu.VMEM((n_z, 8, CH), F32),
        pltpu.VMEM((9, 2, 24, CH), F32),
        pltpu.VMEM((9, 2, 24, CH), F32),
        pltpu.SemaphoreType.DMA((3,)),
        pltpu.SemaphoreType.DMA((19,)),
        pltpu.SemaphoreType.DMA((19,)),
    ]
    features, grad_coarse, grads, grad_lift, grad_land, grad_gain = pl.pallas_call(
        body,
        out_shape=[
            jax.ShapeDtypeStruct((TILE, TILE, CH), BF16),
            jax.ShapeDtypeStruct((1, 1, 2, CIN, CH), F32),
            jax.ShapeDtypeStruct((2, HALF, CH), F32),
            jax.ShapeDtypeStruct((CIN, CH), F32),
            jax.ShapeDtypeStruct((1, CH), F32),
            jax.ShapeDtypeStruct((1, CH), F32),
        ],
        in_specs=[vmem, smem, smem, vmem, vmem, vmem, vmem, anywhere, anywhere, anywhere],
        out_specs=[vmem] * 6,
        scratch_shapes=scratch,
        compiler_params=pltpu.CompilerParams(
            collective_id=0, has_side_effects=True, vmem_limit_bytes=48 << 20
        ),
        name="block",
    )(
        coarse_blocks,
        block_ids,
        quadrant,
        land_mask,
        lift_weight,
        land_vector.reshape(1, CH),
        norm_gain.reshape(1, CH),
        first_weight,
        second_weight,
        cotangent,
    )
    return (
        features,
        grad_coarse,
        grads[1].reshape(TAPS, CH, CH),
        grads[0].reshape(TAPS, CH, CH),
        grad_lift,
        grad_land.reshape(CH),
        grad_gain.reshape(CH),
    )


def solution(mesh):
    in_specs = (
        P("row", "col", None, None, None),
        P("row", "col", None),
        P("row", "col", None),
        P("row", "col"),
        P(),
        P(),
        P(),
        P(),
        P(),
        P("row", "col", None),
    )
    out_specs = (P("row", "col", None), P("row", "col", None, None, None), P(), P(), P(), P(), P())
    return jax.shard_map(shards, mesh=mesh, in_specs=in_specs, out_specs=out_specs, check_vma=False)
```

time: 935 us -> 95.6 us (0.10)
  blocking collectives: 447 us -> 0 us
  waiting for transfers between devices: 336 us -> 0 us
  starting transfers between devices: 86.2 us -> 0 us
  Pallas kernels: 0 us -> 82.9 us
  matrix products: 23.4 us -> 0 us
  between operations: 15.3 us -> 0.65 us
    psum x4 -> x0, blocking collectives: 447 us -> none  [the longest x1 118 us: shards(): lax.psum((gain_term, jnp.sum(grad_normed, axis=(0, 2)), jnp.sum(grad_norm...]
    psum x1 -> x0, waiting for transfers between devices: 328 us -> none  [shards(): grad_first = lax.psum(first_term, ('row', 'col'))]
    ppermute x32 -> x0, starting transfers between devices: 86.2 us -> none  [the longest x12 33.3 us: shifted(): return lax.ppermute(x, axis, pairs)]
    pallas_call x0 -> x1, Pallas kernels: none -> 82.9 us  [shards(): pl.pallas_call(body, out_shape=[jax.ShapeDtypeStruct((TILE, TILE, CH), BF...]
    dot_general x64 -> x0, matrix products: 23.4 us -> none  [the longest x18 7.32 us: apply_taps(): jnp.dot(window.reshape(-1, channels), weight[number].T, preferred_element...]
  transfers between devices with their start and end apart: 33 -> 0, of which waited for: 4 -> 0; matrix products, arithmetic and copies ran while one was open for 2% -> 0% of each run, Pallas kernels for 0% -> 0%
where the time goes in v1:
time: 95.6 us; the launch traced here: 95.2 us
  Pallas kernels  82.9 us (87%)
  local copies, waits for them, and re-layouts  11.6 us (12%)
    pallas_call x1, Pallas kernels, shards(): pl.pallas_call(body, out_shape=[jax.ShapeDtypeStruct((TILE, TILE, CH), BF...  82.9 us
    unnamed x24, local copies, waits for them, and re-layouts  10.5 us

profile of v1, /device:TPU:1, one launch (start us, length us, event | category | flops | bytes accessed | tf_op | source)
XLA Modules:
  0.0 95.2 jit_solution(255556604751747847)
XLA Ops:
  0.6 0.7 copy.17.refs_0_
  1.3 0.0 copy-start
  1.3 1.0 %copy-done = bf16[9,128,128]{2,1,0:T(8,128)(2,1)S(1)} copy-done((bf16[9,128,128]{2,1,0:T(8,128)(2,1)S(1)}, bf16[9,128,128]{2,1,0:T(8,128)(2,1)}, u32[]{:S(2)}) %copy-start) | copy-done | bytes 294936
  2.3 0.0 copy-start.1
  2.3 1.0 %copy-done.1 = bf16[9,128,128]{2,1,0:T(8,128)(2,1)S(1)} copy-done((bf16[9,128,128]{2,1,0:T(8,128)(2,1)S(1)}, bf16[9,128,128]{2,1,0:T(8,128)(2,1)}, u32[]{:S(2)}) %copy-start.1) | copy-done | bytes 294936
  3.3 0.0 copy-start.2
  3.3 0.9 copy-done.2
  4.2 0.0 copy-start.3
  4.2 0.7 copy-done.3
  4.9 0.0 copy-start.4
  4.9 0.7 copy-done.4
  5.6 0.0 copy-start.5
  5.6 0.7 copy-done.5
  6.3 0.0 copy-start.6
  6.3 0.7 copy-done.6
  6.9 0.0 copy-start.7
  6.9 0.7 copy-done.7
  7.6 0.0 copy-start.8
  7.6 0.7 copy-done.8
  8.2 82.9 %block.1 = (bf16[32,32,128]{2,1,0:T(8,128)(2,1)S(1)}, f32[1,1,2,20,128]{4,3,2,1,0:T(8,128)S(1)}, f32[2,1152,128]{2,1,0:T(8,128)S(1)}, f32[20,128]{1,0:T(8,128)S(...) custom-call(bf16[1,1,2,20,128]{4,3,2,1,0:T(8,128)(2,1)S(1)} %copy.17.refs_0_, s32[1,1,6]{2,1,0:T(1,128)S(1)} %copy-done.5, ...), custom_call_target="tpu_custom_call" | custom-call | tf_op jit(solution)/shard_map/block/pallas_call | solution.py:682
  91.2 0.6 copy.18
  91.8 1.1 %fusion = (f32[1,1152,128]{2,1,0:T(8,128)}, f32[1,1152,128]{2,1,0:T(8,128)}) fusion(f32[2,1152,128]{2,1,0:T(8,128)S(1)} %get-tuple-element.15), kind=kLoop, calls=%fused_computation | loop fusion | bytes 2359296 | tf_op jit(solution)/shard_map/slice | solution.py:715
  92.9 0.7 copy.23
  93.6 0.6 copy.24
  94.2 0.5 copy.25
  94.7 0.5 copy.26
Async XLA Ops:
  1.3 1.0 %copy-start = (bf16[9,128,128]{2,1,0:T(8,128)(2,1)S(1)}, bf16[9,128,128]{2,1,0:T(8,128)(2,1)}, u32[]{:S(2)}) copy-start(bf16[9,128,128]{2,1,0:T(8,128)(2,1)} %refs_7_.1) | copy-start | bytes 884740
  2.3 1.0 %copy-start.1 = (bf16[9,128,128]{2,1,0:T(8,128)(2,1)S(1)}, bf16[9,128,128]{2,1,0:T(8,128)(2,1)}, u32[]{:S(2)}) copy-start(bf16[9,128,128]{2,1,0:T(8,128)(2,1)} %refs_8_.1) | copy-start | bytes 884740
  3.3 0.9 copy-start.2
  4.2 0.7 copy-start.3
  4.9 0.7 copy-start.4
  5.6 0.7 copy-start.5
  6.3 0.7 copy-start.6
  6.9 0.7 copy-start.7
  7.6 0.7 copy-start.8

commit v2 on v1

--- a/solution.py
+++ b/solution.py
@@ -111,6 +111,22 @@
 def kernel(
     n_row,
     n_col,
+    coarse_hbm,
+    ids_hbm,
+    quad_hbm,
+    land_hbm,
+    lift_hbm,
+    land_v_hbm,
+    gain_hbm,
+    w1_hbm,
+    w2_hbm,
+    cot_hbm,
+    feat_hbm,
+    gcoarse_hbm,
+    grads_hbm,
+    glift_hbm,
+    gland_hbm,
+    ggain_hbm,
     coarse,
     ids,
     quad,
@@ -118,15 +134,6 @@
     lift_w,
     land_v,
     gain_ref,
-    w1_hbm,
-    w2_hbm,
-    cot_hbm,
-    feat,
-    gcoarse,
-    grads,
-    glift,
-    gland,
-    ggain,
     padf,
     cand,
     up,
@@ -157,15 +164,31 @@
     a2c,
     a2x,
     a2z,
-    a3c,
-    a3x,
-    a3z,
-    gbuf,
-    cbuf,
-    acc,
-    xyb,
+    feat,
+    gcoarse,
+    grads,
+    glift,
+    gland,
+    ggain,
+    long_out,
+    short_out,
+    msend,
+    mrecv,
+    mxy,
+    mown,
+    mz,
+    mall,
+    glong,
+    gshort,
+    clong,
+    cshort,
+    along,
+    ashort,
+    xylong,
+    xyshort,
     zsrc,
     zb,
+    zres,
     ret_s,
     ret_r,
     dma,
@@ -197,14 +220,6 @@
     def waiter(ref, k):
         return remote(ref, ref, snd.at[k], rcv.at[k], core_dev)
 
-    loads = [
-        pltpu.make_async_copy(w1_hbm, w1, dma.at[0]),
-        pltpu.make_async_copy(w2_hbm, w2, dma.at[1]),
-        pltpu.make_async_copy(cot_hbm, cotv, dma.at[2]),
-    ]
-    for load in loads:
-        load.start()
-
     barrier = pltpu.get_barrier_semaphore()
 
     def greet(device, m):
@@ -216,11 +231,38 @@
     for group in (core_g, xy_g, z_g):
         each_other(group, at, greet)
 
+    pairs = [
+        (coarse_hbm, coarse),
+        (lift_hbm, lift_w),
+        (ids_hbm, ids),
+        (quad_hbm, quad),
+        (land_hbm, land),
+        (land_v_hbm, land_v),
+        (gain_hbm, gain_ref),
+        (cot_hbm, cotv),
+        (w2_hbm, w2),
+        (w1_hbm, w1),
+    ]
+    loads = [pltpu.make_async_copy(a, b, dma.at[k]) for k, (a, b) in enumerate(pairs)]
+    for load in loads:
+        load.start()
+
     padf[...] = jnp.zeros_like(padf)
-    padf[0:2, 0:CIN, :] = coarse[0, 0].astype(F32)
+    for load in loads[:2]:
+        load.wait()
+    for m in range(2):
+        padf[m, 0:CIN, :] = coarse[:, m, :].astype(F32)
     padf[2, 0:CIN, :] = lift_w[...].astype(F32)
     cand[4] = padf[0:2].astype(BF16)
 
+    pl.semaphore_wait(barrier, 8 + 1 + n_xy - 1 + n_z - 1)
+
+    for s, (dr, dc) in enumerate(around):
+        if s != 4:
+            remote(cand.at[4], cand.at[8 - s], snd.at[0], rcv.at[0], near(dr, dc)).start()
+
+    for load in loads[2:]:
+        load.wait()
     codes = []
     for k in range(ids.shape[2]):
         block = ids[0, 0, k]
@@ -237,12 +279,6 @@
         return total
 
     weight = {(q, s, m): picks(q, s, m) for q in range(2) for s in range(9) for m in range(2)}
-
-    pl.semaphore_wait(barrier, 8 + 1 + n_xy - 1 + n_z - 1)
-
-    for s, (dr, dc) in enumerate(around):
-        if s != 4:
-            remote(cand.at[4], cand.at[8 - s], snd.at[0], rcv.at[0], near(dr, dc)).start()
 
     fine = lax.broadcasted_iota(jnp.int32, (CH, 512), 1)
     cell = lax.broadcasted_iota(jnp.int32, (CH, 512), 0)
@@ -269,8 +305,6 @@
         gic[edge] = jnp.zeros((WIDE, CH), BF16)
         gig[edge] = jnp.zeros((WIDE, CH), BF16)
 
-    for load in loads:
-        load.wait()
     for k in range(TAPS):
         wt1[:, k * CH : (k + 1) * CH] = w1[8 - k]
         wt2[:, k * CH : (k + 1) * CH] = w2[8 - k]
@@ -428,33 +462,74 @@
 
     loop(2, hidden_rows)
 
-    def tap_grads(x3, gi, half):
+    def tap_grads(x3, gi, half, us):
         length = (ROWS - 2) * WIDE
         grad = jnp.concatenate(
-            [gi[2 - u : 2 - u + ROWS - 2].reshape(length, CH) for u in range(3)], axis=1
+            [gi[2 - u : 2 - u + ROWS - 2].reshape(length, CH) for u in us], axis=1
         )
         out = dot_tn(x3[1 : ROWS - 1].reshape(length, 3 * CH), grad)
-        for u in range(3):
+        for n, u in enumerate(us):
             for v in range(3):
-                gbuf[half, (3 * u + v) * CH : (3 * u + v + 1) * CH, :] = out[
-                    v * CH : (v + 1) * CH, u * CH : (u + 1) * CH
+                to, first = (glong, 3 * u + v) if u < 2 else (gshort, v)
+                to[half, first * CH : (first + 1) * CH, :] = out[
+                    v * CH : (v + 1) * CH, n * CH : (n + 1) * CH
                 ]
 
-    tap_grads(x3b, gic, 0)
-    tap_grads(x3a, gig, 1)
-
-    swap = remote(gbuf.at[1 - core], cbuf, snd.at[6], rcv.at[6], core_dev)
-    swap.start()
+    tap_grads(x3b, gic, 0, (0, 1))
+    tap_grads(x3a, gig, 1, (0, 1))
+    swap_long = remote(glong.at[1 - core], clong, snd.at[6], rcv.at[6], core_dev)
+    swap_long.start()
+    tap_grads(x3b, gic, 0, (2,))
+    tap_grads(x3a, gig, 1, (2,))
+    swap_short = remote(gshort.at[1 - core], cshort, snd.at[7], rcv.at[7], core_dev)
+    swap_short.start()
+
+    inner = slice(LEFT, LEFT + TILE)
+    written = []
+
+    def write_out(src, dst):
+        written.append(pltpu.make_async_copy(src, dst, dma.at[10 + len(written)]))
+        written[-1].start()
+
+    def out_rows(i):
+        first = 2 + i * 16
+        out = dot(windows(x3b, first, 16), w2[...].reshape(HALF, CH)).reshape(16, WIDE, CH)
+        feat[pl.ds(i * 16, 16)] = (ext[0, pl.ds(first, 16), inner, :] + out[:, inner, :]).astype(BF16)
+
+    out_rows(0)
+
+    def share_out(mine, theirs, to, landing, k):
+        def add(m, carry):
+            rows = pl.ds(pl.multiple_of(m * mine.shape[1] // n_xy, 8), mine.shape[1] // n_xy)
+            total = mine[core, rows, :] + theirs[rows, :]
+            to[m] = total
+            return carry
+
+        lax.fori_loop(0, n_xy, add, 0)
+
+        def send(device, m):
+            remote(to.at[m], landing.at[xy], snd.at[k], rcv.at[k], device).start()
+
+        each_other(xy_g, at, send)
+        landing[xy] = to[xy]
+
+    swap_long.wait_recv()
+    share_out(glong, clong, along, xylong, 8)
+    swap_short.wait_recv()
+    share_out(gshort, cshort, ashort, xyshort, 9)
 
     def back_rows(i, sums):
         first = 2 + i * 8
-        inner = slice(LEFT, LEFT + TILE)
         grad_act = dot_nt(windows(x3g, first, 8), wt1[...]).reshape(8, WIDE, CH)[:, inner, :]
         normed = (ext[0, pl.ds(first, 8), inner, :] - group_mean[None]) * inv_spread[None]
         scaled = normed * gain[None]
         gate = sigmoid(scaled)
         grad = grad_act * (gate * (1.0 + scaled * (1.0 - gate)))
         gsc[pl.ds(i * 8, 8)] = grad
+        straight = inv_spread[None] * (grad * gain[None]) + ext[1, pl.ds(first, 8), inner, :]
+        spot = pl.ds(pl.multiple_of(i * 256, 256), 256)
+        for k, part in enumerate(split_two(straight.reshape(256, CH)) + split_two(normed.reshape(256, CH))):
+            glb[spot, k * CH : (k + 1) * CH] = part
         plain, cross = sums
         return (
             plain + jnp.sum(grad.reshape(32, 8, CH), axis=0),
@@ -466,39 +541,50 @@
     both = jnp.concatenate(
         [jnp.sum(plain, axis=0, keepdims=True), jnp.sum(cross, axis=0, keepdims=True)], axis=0
     )
-    start_level(core_g, a2c, 7, both)
-
-    swap.wait_recv()
-    acc[...] = gbuf[core] + cbuf[...]
-    share = HALF // n_xy
-
-    def share_of(ref, m):
-        return ref.at[pl.ds(pl.multiple_of(m * share, 8), share)]
-
-    def send_share(device, m):
-        remote(share_of(acc, m), xyb.at[xy], snd.at[8], rcv.at[8], device).start()
-
-    start_level(xy_g, a2x, 9, add_up(end_level(a2c, 7)))
-    each_other(xy_g, at, send_share)
-    xyb[xy] = acc[pl.ds(pl.multiple_of(xy * share, 8), share), :]
-
-    def out_rows(i):
-        first = 2 + i * 16
-        inner = slice(LEFT, LEFT + TILE)
-        out = dot(windows(x3b, first, 16), w2[...].reshape(HALF, CH)).reshape(16, WIDE, CH)
-        feat[pl.ds(i * 16, 16)] = (ext[0, pl.ds(first, 16), inner, :] + out[:, inner, :]).astype(BF16)
-
-    loop(2, out_rows)
-
-    start_level(z_g, a2z, 10, add_up(end_level(a2x, 9)))
-
-    waiter(xyb.at[pl.ds(0, n_xy - 1)], 8).wait()
-    zsrc[...] = add_up([xyb[i] for i in range(n_xy)])
-    tiles = share // 8
+    start_level(core_g, a2c, 10, both)
+
+    which = lax.broadcasted_iota(jnp.int32, (24, CH), 0)
+    lane = lax.broadcasted_iota(jnp.int32, (24, CH), 1)
+    field_rows = dot(ft[...], glb[...])
+
+    def by_field(k):
+        part = field_rows[:, k * CH : (k + 1) * CH] + field_rows[:, (k + 1) * CH : (k + 2) * CH]
+        on_land = jnp.sum(part[32:64], axis=0, keepdims=True)
+        return jnp.where(which == CIN, on_land, part[0:24])
+
+    alone = dot_nt(jnp.full((8, PIX), 1.0, BF16), ft[...])[0:1]
+    msend[0] = by_field(0)
+    msend[1] = jnp.where(which == CIN + 1, alone, by_field(2))
+    m_swap = remote(msend.at[1 - core], mrecv, snd.at[13], rcv.at[13], core_dev)
+    m_swap.start()
+
+    out_rows(1)
+    write_out(feat, feat_hbm)
+
+    start_level(xy_g, a2x, 11, add_up(end_level(a2c, 10)))
+
+    goals = [(5 * t + 8 * core + 1) & (n_xy - 1) for t in range(3)]
+    held = [goal == xy for goal in goals]
+    holder = held[0] | held[1] | held[2]
+
+    m_swap.wait_recv()
+    mown[...] = msend[core] + mrecv[...]
+    for t in range(3):
+        strip = mown.at[8 * t : 8 * t + 8]
+
+        @pl.when(jnp.logical_not(held[t]))
+        def _():
+            remote(strip, mxy.at[xy], snd.at[14], rcv.at[14], member_of(xy_g, at, goals[t])).start()
+
+        @pl.when(held[t])
+        def _():
+            mxy[xy] = mown[8 * t : 8 * t + 8]
+
+    long_rows = glong.shape[1] // n_xy
+    long_tiles = long_rows // 8
+    tiles = zsrc.shape[0] // 8
     turn = (xy + 8 * core) & (n_z - 1)
     mine = (z - turn) & (n_z - 1)
-    owner = mine < tiles
-    strip = pl.ds(pl.multiple_of(jnp.minimum(mine, tiles - 1) * 8, 8), 8)
 
     def send_tile(t, carry):
         goal = (t + turn) & (n_z - 1)
@@ -508,36 +594,65 @@
             remote(
                 zsrc.at[pl.ds(pl.multiple_of(t * 8, 8), 8)],
                 zb.at[z],
-                snd.at[11],
-                rcv.at[11],
+                snd.at[16],
+                rcv.at[16],
                 member_of(z_g, at, goal),
             ).start()
 
         return carry
 
-    lax.fori_loop(0, tiles, send_tile, 0)
-
-    totals = add_up(end_level(a2z, 10))
+    waiter(xylong.at[pl.ds(0, n_xy - 1)], 8).wait_recv()
+    zsrc[0:long_rows] = add_up([xylong[i] for i in range(n_xy)])
+    lax.fori_loop(0, long_tiles, send_tile, 0)
+    waiter(xyshort.at[pl.ds(0, n_xy - 1)], 9).wait_recv()
+    zsrc[long_rows:] = add_up([xyshort[i] for i in range(n_xy)])
+    lax.fori_loop(long_tiles, tiles, send_tile, 0)
+
+    start_level(z_g, a2z, 12, add_up(end_level(a2x, 11)))
+
+    @pl.when(holder)
+    def _():
+        waiter(mxy.at[pl.ds(0, n_xy - 1)], 14).wait_recv()
+        start_level(z_g, mz, 15, add_up([mxy[i] for i in range(n_xy)]))
+
+    spot = pl.ds(pl.multiple_of(jnp.minimum(mine, tiles - 1) * 8, 8), 8)
+
+    def whole_tile(k):
+        zb[z] = zsrc[spot, :]
+        waiter(zb.at[pl.ds(0, n_z - 1)], 16).wait_recv()
+        zres[spot, :] = add_up([zb[i] for i in range(n_z)]) * report
+
+        def send(device, m):
+            remote(zres.at[spot], zres.at[spot], snd.at[17], rcv.at[k], device).start()
+
+        each_other(z_g, at, send)
+
+    in_long = mine < long_tiles
+    in_short = (mine >= long_tiles) & (mine < tiles)
+    owner = mine < tiles
+
+    @pl.when(in_long)
+    def _():
+        whole_tile(17)
+
+    @pl.when(in_short)
+    def _():
+        whole_tile(18)
+
+    totals = add_up(end_level(a2z, 12))
     ggain[...] = totals[1:2] * report
+    write_out(ggain, ggain_hbm)
     plain_sum = group_sums(totals[0:1] * gain) * (1.0 / members)
     cross_sum = group_sums(totals[1:2] * gain) * (1.0 / members)
 
     def lifted_rows(i):
         first = 2 + i * 8
-        inner = slice(LEFT, LEFT + TILE)
         normed = (ext[0, pl.ds(first, 8), inner, :] - group_mean[None]) * inv_spread[None]
         grad = gsc[pl.ds(i * 8, 8)] * gain[None] - plain_sum[None] - normed * cross_sum[None]
         grad = inv_spread[None] * grad + ext[1, pl.ds(first, 8), inner, :]
-        hi, lo = split_two(grad.reshape(256, CH))
-        spot = pl.ds(pl.multiple_of(i * 256, 256), 256)
-        glb[spot, 0:CH] = hi
-        glb[spot, CH:] = lo
+        glb[pl.ds(pl.multiple_of(i * 256, 256), 256), 0:CH] = grad.reshape(256, CH).astype(BF16)
 
     loop(4, lifted_rows)
-    both = dot(ft[...], glb[...])
-    on_land = jnp.sum(both[32:64, 0:CH] + both[32:64, CH:], axis=0, keepdims=True)
-    which = lax.broadcasted_iota(jnp.int32, (24, CH), 0)
-    start_level(core_g, a3c, 12, jnp.where(which == CIN, on_land, both[0:24, 0:CH]))
 
     fine_hi, fine_lo = split_two(dot_nt(wext[0:32], glb[:, 0:CH]))
     stacked = jnp.concatenate(
@@ -548,67 +663,152 @@
     for s, (dr, dc) in enumerate(around):
         for m in range(2):
             ret_s[s, m] = weight[0, s, m] * lowered[0:24] + weight[1, s, m] * lowered[32:56]
-
-    start_level(xy_g, a3x, 13, add_up(end_level(a3c, 12)))
-    for s, (dr, dc) in enumerate(around):
         if s != 4:
-            remote(ret_s.at[s], ret_r.at[8 - s], snd.at[14], rcv.at[14], near(dr, dc)).start()
-
-    @pl.when(owner)
+            remote(ret_s.at[s], ret_r.at[8 - s], snd.at[19], rcv.at[19], near(dr, dc)).start()
+
+    @pl.when(holder)
     def _():
-        zb[z] = zsrc[strip, :]
-        waiter(zb.at[pl.ds(0, n_z - 1)], 11).wait_recv()
-        waiter(zsrc.at[pl.ds(0, share - 8)], 11).wait_send()
-        whole = add_up([zb[i] for i in range(n_z)]) * report
-        spot = pl.ds(pl.multiple_of(xy * share + mine * 8, 8), 8)
-        grads[core, spot, :] = whole
-
-        def send_whole(device, m):
-            piece = grads.at[core, spot]
-            remote(piece, piece, snd.at[15], rcv.at[15], device).start()
-
-        each_other(z_g, at, send_whole)
-
-    @pl.when(jnp.logical_not(owner))
-    def _():
-        waiter(zsrc, 11).wait_send()
-
-    start_level(z_g, a3z, 16, add_up(end_level(a3x, 13)))
-
-    @pl.when(owner)
-    def _():
-        waiter(zb.at[pl.ds(0, n_z - 1)], 15).wait_send()
-        waiter(zsrc.at[pl.ds(0, share - 8)], 15).wait_recv()
-
-    @pl.when(jnp.logical_not(owner))
-    def _():
-        waiter(zsrc, 15).wait_recv()
-
-    here = grads.at[core, pl.ds(pl.multiple_of(xy * share, 8), share)]
-
-    def send_back(device, m):
-        remote(here, here, snd.at[17], rcv.at[17], device).start()
-
-    each_other(xy_g, at, send_back)
-
-    waiter(ret_r.at[pl.ds(0, 8)], 14).wait()
+        waiter(mz.at[pl.ds(0, n_z - 1)], 15).wait()
+
+    for t in range(3):
+        place = mall.at[core, 8 * t : 8 * t + 8]
+
+        @pl.when(held[t])
+        def _():
+            mall[core, 8 * t : 8 * t + 8, :] = add_up([mz[i] for i in range(n_z)])
+
+            def send(device, m):
+                remote(place, place, snd.at[20], rcv.at[20], device).start()
+
+            each_other(xy_g, at, send)
+
+    def wait_tiles(count, mine_too, k):
+        @pl.when(mine_too)
+        def _():
+            waiter(zres.at[pl.ds(0, (count - 1) * 8)], k).wait_recv()
+
+        @pl.when(jnp.logical_not(mine_too))
+        def _():
+            waiter(zres.at[pl.ds(0, count * 8)], k).wait_recv()
+
+    def send_shares(out, k):
+        piece = out.at[core, xy]
+
+        def send(device, m):
+            remote(piece, piece, snd.at[k], rcv.at[k], device).start()
+
+        each_other(xy_g, at, send)
+
+    wait_tiles(long_tiles, in_long, 17)
+    long_out[core, xy] = zres[0:long_rows].astype(BF16)
+    send_shares(long_out, 21)
+    wait_tiles(tiles - long_tiles, in_short, 18)
+    rest = zres[long_rows:]
+    short_out[core, xy] = jnp.concatenate([rest, jnp.zeros((short_out.shape[2] - rest.shape[0], CH), F32)], axis=0).astype(BF16)
+    send_shares(short_out, 22)
+
+    waiter(ret_r.at[pl.ds(0, 8)], 19).wait()
     for m in range(2):
         total = ret_s[4, m]
         for s in range(9):
             if s != 4:
                 total = total + ret_r[s, m]
-        gcoarse[0, 0, m] = total[0:CIN]
-
-    totals = add_up(end_level(a3z, 16)) * report
-    glift[...] = totals[0:CIN]
-    gland[...] = totals[CIN : CIN + 1]
-
-    waiter(xyb.at[pl.ds(0, n_xy - 1)], 17).wait()
-    half = remote(grads.at[core], grads.at[core], snd.at[18], rcv.at[18], core_dev)
-    half.start()
+        gcoarse[:, m, :] = total[0:CIN]
+    write_out(gcoarse, gcoarse_hbm)
+
+    @pl.when(holder)
+    def _():
+        waiter(mall.at[core, 0:16], 20).wait_recv()
+
+    @pl.when(jnp.logical_not(holder))
+    def _():
+        waiter(mall.at[core], 20).wait_recv()
+
+    m_back = remote(mall.at[core], mall.at[core], snd.at[23], rcv.at[23], core_dev)
+    m_back.start()
+
+    long_all = n_xy * long_rows
+    short_rows = zsrc.shape[0] - long_rows
+
+    def widen_long(half):
+        grads[half, 0:long_all, :] = long_out[half].astype(F32).reshape(long_all, CH)
+        piece = (half, pl.ds(0, long_all))
+        write_out(grads.at[piece], grads_hbm.at[piece])
+
+    def widen_short(half):
+        part = short_out[half][:, 0:short_rows, :].astype(F32)
+        grads[half, long_all:, :] = part.reshape(n_xy * short_rows, CH)
+        piece = (half, pl.ds(long_all, n_xy * short_rows))
+        write_out(grads.at[piece], grads_hbm.at[piece])
+
+    waiter(long_out.at[core, pl.ds(0, n_xy - 1)], 21).wait_recv()
+    back_long = remote(long_out.at[core], long_out.at[core], snd.at[24], rcv.at[24], core_dev)
+    back_long.start()
+    widen_long(core)
+
+    m_back.wait()
+    straight, crossed = mall[0], mall[1]
+    fields = ((lane == which) & (which < CIN)) | ((which == CIN) & (lane >= 32) & (lane < 64))
+    alone = jnp.sum(jnp.where(fields, crossed[CIN + 1 : CIN + 2], 0.0), axis=1, keepdims=True)
+    lift_all = straight - (inv_spread * plain_sum) * alone - (inv_spread * cross_sum) * crossed
+    lift_all = lift_all * report
+    glift[...] = lift_all[0:CIN]
+    gland[...] = lift_all[CIN : CIN + 1]
+    write_out(glift, glift_hbm)
+    write_out(gland, gland_hbm)
+
+    waiter(short_out.at[core, pl.ds(0, n_xy - 1)], 22).wait_recv()
+    back_short = remote(short_out.at[core], short_out.at[core], snd.at[25], rcv.at[25], core_dev)
+    back_short.start()
+    widen_short(core)
+
     waiter(cand.at[pl.ds(0, 8)], 0).wait_send()
-    swap.wait_send()
-    half.wait()
+    swap_long.wait_send()
+    swap_short.wait_send()
+    m_swap.wait_send()
+    waiter(xylong.at[pl.ds(0, n_xy - 1)], 8).wait_send()
+    waiter(xyshort.at[pl.ds(0, n_xy - 1)], 9).wait_send()
+    waiter(long_out.at[core, pl.ds(0, n_xy - 1)], 21).wait_send()
+    waiter(short_out.at[core, pl.ds(0, n_xy - 1)], 22).wait_send()
+
+    @pl.when(holder)
+    def _():
+        waiter(mown.at[0:16], 14).wait_send()
+        waiter(mxy.at[pl.ds(0, n_xy - 1)], 20).wait_send()
+
+    @pl.when(jnp.logical_not(holder))
+    def _():
+        waiter(mown, 14).wait_send()
+
+    @pl.when(owner)
+    def _():
+        waiter(zsrc.at[pl.ds(0, (tiles - 1) * 8)], 16).wait_send()
+        waiter(zb.at[pl.ds(0, n_z - 1)], 17).wait_send()
+
+    @pl.when(jnp.logical_not(owner))
+    def _():
+        waiter(zsrc, 16).wait_send()
+
+    back_long.wait()
+    widen_long(1 - core)
+    back_short.wait()
+    widen_short(1 - core)
+    for copy in written:
+        copy.wait()
+
+
+def finish(feat, gcoarse, grads, glift, gland, ggain, *rest):
+    outs, held, dma = rest[:7], rest[7:14], rest[14]
+    sources = (grads.at[1], grads.at[0], feat, gcoarse, glift, gland, ggain)
+    ins = [pltpu.make_async_copy(a, b, dma.at[0, k]) for k, (a, b) in enumerate(zip(sources, held))]
+    for copy in ins:
+        copy.start()
+    copies = [pltpu.make_async_copy(a, b, dma.at[1, k]) for k, (a, b) in enumerate(zip(held, outs))]
+    for arrived, copy in zip(ins, copies):
+        arrived.wait()
+        copy.start()
+    for copy in copies:
+        copy.wait()
 
 
 def shards(*args):
@@ -630,10 +830,26 @@
     def body(*refs):
         kernel(n_row, n_col, *refs)
 
-    vmem = pl.BlockSpec(memory_space=pltpu.VMEM)
-    smem = pl.BlockSpec(memory_space=pltpu.SMEM)
-    anywhere = pl.BlockSpec(memory_space=pl.ANY)
+    hbm = pl.BlockSpec(memory_space=pltpu.HBM)
+    rows_long = 6 * CH // n_xy
+    rows_short = 3 * CH // n_xy
+    pad_short = -(-rows_short // 16) * 16
+    results = [
+        jax.ShapeDtypeStruct((TILE, TILE, CH), BF16),
+        jax.ShapeDtypeStruct((CIN, 2, CH), F32),
+        jax.ShapeDtypeStruct((2, HALF, CH), F32),
+        jax.ShapeDtypeStruct((CIN, CH), F32),
+        jax.ShapeDtypeStruct((1, CH), F32),
+        jax.ShapeDtypeStruct((1, CH), F32),
+    ]
     scratch = [
+        pltpu.VMEM((CIN, 2, CH), BF16),
+        pltpu.SMEM(block_ids.shape, jnp.int32),
+        pltpu.SMEM(quadrant.shape, jnp.int32),
+        pltpu.VMEM((TILE, TILE), jnp.int32),
+        pltpu.VMEM((CIN, CH), BF16),
+        pltpu.VMEM((1, CH), F32),
+        pltpu.VMEM((1, CH), F32),
         pltpu.VMEM((3, 32, CH), F32),
         pltpu.VMEM((9, 2, 32, CH), BF16),
         pltpu.VMEM((CH, 512), BF16),
@@ -657,47 +873,56 @@
         pltpu.VMEM((ROWS, WIDE, CH), BF16),
         pltpu.VMEM((ROWS, WIDE, CH), F32),
         pltpu.VMEM((TILE, TILE, CH), F32),
-        pltpu.VMEM((PIX, 2 * CH), BF16),
+        pltpu.VMEM((PIX, 4 * CH), BF16),
         pltpu.VMEM((2, 2, CH), F32),
         pltpu.VMEM((n_xy, 2, CH), F32),
         pltpu.VMEM((n_z, 2, CH), F32),
         pltpu.VMEM((2, 2, CH), F32),
         pltpu.VMEM((n_xy, 2, CH), F32),
         pltpu.VMEM((n_z, 2, CH), F32),
+        pltpu.VMEM((TILE, TILE, CH), BF16),
+        pltpu.VMEM((CIN, 2, CH), F32),
+        pltpu.VMEM((2, HALF, CH), F32),
+        pltpu.VMEM((CIN, CH), F32),
+        pltpu.VMEM((1, CH), F32),
+        pltpu.VMEM((1, CH), F32),
+        pltpu.VMEM((2, n_xy, rows_long, CH), BF16),
+        pltpu.VMEM((2, n_xy, pad_short, CH), BF16),
         pltpu.VMEM((2, 24, CH), F32),
-        pltpu.VMEM((n_xy, 24, CH), F32),
-        pltpu.VMEM((n_z, 24, CH), F32),
-        pltpu.VMEM((2, HALF, CH), F32),
-        pltpu.VMEM((HALF, CH), F32),
-        pltpu.VMEM((HALF, CH), F32),
-        pltpu.VMEM((n_xy, HALF // n_xy, CH), F32),
-        pltpu.VMEM((HALF // n_xy, CH), F32),
+        pltpu.VMEM((24, CH), F32),
+        pltpu.VMEM((n_xy, 8, CH), F32),
+        pltpu.VMEM((24, CH), F32),
         pltpu.VMEM((n_z, 8, CH), F32),
+        pltpu.VMEM((2, 24, CH), F32),
+        pltpu.VMEM((2, 6 * CH, CH), F32),
+        pltpu.VMEM((2, 3 * CH, CH), F32),
+        pltpu.VMEM((6 * CH, CH), F32),
+        pltpu.VMEM((3 * CH, CH), F32),
+        pltpu.VMEM((n_xy, rows_long, CH), F32),
+        pltpu.VMEM((n_xy, rows_short, CH), F32),
+        pltpu.VMEM((n_xy, rows_long, CH), F32),
+        pltpu.VMEM((n_xy, rows_short, CH), F32),
+        pltpu.VMEM((rows_long + rows_short, CH), F32),
+        pltpu.VMEM((n_z, 8, CH), F32),
+        pltpu.VMEM((rows_long + rows_short, CH), F32),
         pltpu.VMEM((9, 2, 24, CH), F32),
         pltpu.VMEM((9, 2, 24, CH), F32),
-        pltpu.SemaphoreType.DMA((3,)),
         pltpu.SemaphoreType.DMA((19,)),
-        pltpu.SemaphoreType.DMA((19,)),
+        pltpu.SemaphoreType.DMA((26,)),
+        pltpu.SemaphoreType.DMA((26,)),
     ]
-    features, grad_coarse, grads, grad_lift, grad_land, grad_gain = pl.pallas_call(
+    parts = pl.pallas_call(
         body,
-        out_shape=[
-            jax.ShapeDtypeStruct((TILE, TILE, CH), BF16),
-            jax.ShapeDtypeStruct((1, 1, 2, CIN, CH), F32),
-            jax.ShapeDtypeStruct((2, HALF, CH), F32),
-            jax.ShapeDtypeStruct((CIN, CH), F32),
-            jax.ShapeDtypeStruct((1, CH), F32),
-            jax.ShapeDtypeStruct((1, CH), F32),
-        ],
-        in_specs=[vmem, smem, smem, vmem, vmem, vmem, vmem, anywhere, anywhere, anywhere],
-        out_specs=[vmem] * 6,
+        out_shape=results,
+        in_specs=[hbm] * 10,
+        out_specs=[hbm] * 6,
         scratch_shapes=scratch,
         compiler_params=pltpu.CompilerParams(
-            collective_id=0, has_side_effects=True, vmem_limit_bytes=48 << 20
+            collective_id=0, has_side_effects=True, vmem_limit_bytes=60 << 20
         ),
         name="block",
     )(
-        coarse_blocks,
+        jnp.transpose(coarse_blocks[0, 0], (1, 0, 2)),
         block_ids,
         quadrant,
         land_mask,
@@ -708,11 +933,23 @@
         second_weight,
         cotangent,
     )
+    wide = jax.ShapeDtypeStruct((HALF, CH), F32)
+    outputs = [wide, wide, results[0], results[1]] + results[3:]
+    grad_first, grad_second, features, grad_coarse, grad_lift, grad_land, grad_gain = pl.pallas_call(
+        finish,
+        out_shape=outputs,
+        in_specs=[hbm] * 6,
+        out_specs=[hbm] * 7,
+        scratch_shapes=[pltpu.VMEM(out.shape, out.dtype) for out in outputs]
+        + [pltpu.SemaphoreType.DMA((2, 7))],
+        compiler_params=pltpu.CompilerParams(vmem_limit_bytes=60 << 20),
+        name="finish",
+    )(*parts)
     return (
         features,
-        grad_coarse,
-        grads[1].reshape(TAPS, CH, CH),
-        grads[0].reshape(TAPS, CH, CH),
+        jnp.transpose(grad_coarse, (1, 0, 2))[None, None],
+        grad_first.reshape(TAPS, CH, CH),
+        grad_second.reshape(TAPS, CH, CH),
         grad_lift,
         grad_land.reshape(CH),
         grad_gain.reshape(CH),

time: 95.6 us -> 78.2 us (0.82)
  local copies, waits for them, and re-layouts: 11.6 us -> 0 us
  Pallas kernels: 82.9 us -> 77.4 us
    unnamed x24 -> x0, local copies, waits for them, and re-layouts: 10.5 us -> none
    pallas_call x1 -> x2, Pallas kernels: 82.9 us -> 77.4 us  [the longest x1 75.2 us: shards(): pl.pallas_call(body, out_shape=results, in_specs=[hbm] * 10, out_specs=[h...]
    slice x1 -> x0, local copies, waits for them, and re-layouts: 1.08 us -> none  [shards(): grads[0].reshape(TAPS, CH, CH)]
where the time goes in v2:
time: 78.2 us; the launch traced here: 78.1 us
  Pallas kernels  77.4 us (99%)
    pallas_call x1, Pallas kernels, shards(): pl.pallas_call(body, out_shape=results, in_specs=[hbm] * 10, out_specs=[h...  75.2 us
    pallas_call x1, Pallas kernels, shards(): pl.pallas_call(finish, out_shape=outputs, in_specs=[hbm] * 6, out_specs=[...  2.29 us

profile of v2, /device:TPU:1, one launch (start us, length us, event | category | flops | bytes accessed | tf_op | source)
XLA Modules:
  0.0 78.1 jit_solution(5934063463615050895)
XLA Ops:
  0.6 75.2 %block.1 = (bf16[32,32,128]{2,1,0:T(8,128)(2,1)}, f32[20,2,128]{2,1,0:T(2,128)}, f32[2,1152,128]{2,1,0:T(8,128)}, f32[20,128]{1,0:T(8,128)}, f32[1,128]{1,0:T(1,128)}, /*index=5*/f32[1,128]{1,0:T(1,128)}) custom-call(bf16[20,2,128]{2,1,0:T(2,128)(2,1)} %bitcast.12, s32[1,1,6]{2,1,0:T(1,128)} %refs_1_.1, s32[1,1,6]{2,1,0:T(1,128)} %refs_2_.1, ...), custom_call_target="tpu_custom_call" | custom-call | tf_op jit(solution)/shard_map/block/pallas_call | solution.py:914
  75.8 2.3 %finish.1 = (f32[1152,128]{1,0:T(8,128)}, f32[1152,128]{1,0:T(8,128)}, bf16[32,32,128]{2,1,0:T(8,128)(2,1)}, f32[20,2,128]{2,1,0:T(2,128)}, f32[20,128]{1,0:T(8,...) custom-call(bf16[32,32,128]{2,1,0:T(8,128)(2,1)} %get-tuple-element.20.feat, f32[20,2,128]{2,1,0:T(2,128)} %get-tuple-element.21.gcoarse, ...), custom_call_target="tpu_custom_call" | custom-call | tf_op jit(solution)/shard_map/finish/pallas_call | solution.py:938

commit v3 on v2

--- a/solution.py
+++ b/solution.py
@@ -21,6 +21,10 @@
 CIN = 20
 PIX = TILE * TILE
 TAPS = 9
+FAR_FIRST = tuple(
+    sum(step << (4 * k) for k, step in enumerate(half))
+    for half in ((5, 3, 7, 12, 13, 1, 4, 2), (10, 11, 14, 15, 6, 8, 9))
+)
 HALF = TAPS * CH
 
 
@@ -54,13 +58,19 @@
 def each_other(group, at, act):
     n = size_of(group)
     me = place_in(group, at)
+    flat = len(group) == 2 and n == 16
 
     def body(k, carry):
-        m = (me + k) & (n - 1)
+        if flat:
+            step = jnp.where(k < 8, FAR_FIRST[0], FAR_FIRST[1])
+            m = me ^ ((step >> ((k & 7) * 4)) & 15)
+        else:
+            away = (k + 1) >> 1
+            m = (me + n // 2 + jnp.where((k & 1) == 1, away, -away) + n) & (n - 1)
         act(member_of(group, at, m), m)
         return carry
 
-    lax.fori_loop(1, n, body, 0)
+    lax.fori_loop(0, n - 1, body, 0)
 
 
 def remote(src, dst, send, recv, device):
@@ -149,12 +159,10 @@
     rh_r,
     ch_s,
     ch_r,
-    x3a,
-    x3b,
+    x3ab,
     x3c,
     x3g,
-    gic,
-    gig,
+    gi,
     t2,
     gsc,
     glb,
@@ -211,6 +219,8 @@
     xy = place_in(xy_g, at)
     z = place_in(z_g, at)
     core_dev = member_of(core_g, at, 1 - core)
+    x3b, x3a = x3ab.at[0], x3ab.at[1]
+    gic, gig = gi.at[0], gi.at[1]
 
     def near(dr, dc):
         return ((row + dr + n_row) & (n_row - 1), (col + dc + n_col) & (n_col - 1))
@@ -302,13 +312,39 @@
     for lo, hi in ((0, LEFT), (LEFT + TILE, WIDE)):
         ext[:, :, lo:hi, :] = jnp.zeros((2, ROWS, 8, CH), F32)
     for edge in (0, ROWS - 1):
-        gic[edge] = jnp.zeros((WIDE, CH), BF16)
-        gig[edge] = jnp.zeros((WIDE, CH), BF16)
+        gi[:, edge] = jnp.zeros((2, WIDE, CH), BF16)
 
     for k in range(TAPS):
         wt1[:, k * CH : (k + 1) * CH] = w1[8 - k]
         wt2[:, k * CH : (k + 1) * CH] = w2[8 - k]
     ext[1, 2 : 2 + TILE, LEFT : LEFT + TILE, :] = cotv[...].astype(F32)
+
+    def pack_rows(a):
+        rh_s[a, 0] = ext[a, 2:4, LEFT : LEFT + TILE, :]
+        rh_s[a, 1] = ext[a, TILE : TILE + 2, LEFT : LEFT + TILE, :]
+
+    def send_rows(a, k):
+        for side, step in ((0, -1), (1, 1)):
+            remote(rh_s.at[a, side], rh_r.at[a, side], snd.at[k], rcv.at[k], near(step, 0)).start()
+
+    def rows_to_columns(a, k_rows, k_cols):
+        waiter(rh_r.at[a], k_rows).wait()
+        ext[a, 2 + TILE : 4 + TILE, LEFT : LEFT + TILE, :] = rh_r[a, 0]
+        ext[a, 0:2, LEFT : LEFT + TILE, :] = rh_r[a, 1]
+        for k in range(2):
+            ch_s[a, 0, k, 0:ROWS, :] = ext[a, :, LEFT + k, :]
+            ch_s[a, 1, k, 0:ROWS, :] = ext[a, :, LEFT + TILE - 2 + k, :]
+        for side, step in ((0, -1), (1, 1)):
+            remote(ch_s.at[a, side], ch_r.at[a, side], snd.at[k_cols], rcv.at[k_cols], near(0, step)).start()
+
+    def put_columns(a, k_cols):
+        waiter(ch_r.at[a], k_cols).wait()
+        for k in range(2):
+            ext[a, :, LEFT + TILE + k, :] = ch_r[a, 0, k, 0:ROWS, :]
+            ext[a, :, LEFT - 2 + k, :] = ch_r[a, 1, k, 0:ROWS, :]
+
+    pack_rows(1)
+    send_rows(1, 27)
 
     waiter(cand.at[pl.ds(0, 8)], 0).wait_recv()
     sums = []
@@ -355,31 +391,17 @@
 
     start_level(core_g, a1c, 1, jnp.concatenate([mean_here, square_here], axis=0))
 
-    rh_s[0] = ext[:, 2:4, LEFT : LEFT + TILE, :]
-    rh_s[1] = ext[:, TILE : TILE + 2, LEFT : LEFT + TILE, :]
+    pack_rows(0)
+    rows_to_columns(1, 27, 28)
 
     moments = merge(end_level(a1c, 1), float(PIX))
     start_level(xy_g, a1x, 2, moments)
-    remote(rh_s.at[0], rh_r.at[0], snd.at[4], rcv.at[4], near(-1, 0)).start()
-    remote(rh_s.at[1], rh_r.at[1], snd.at[4], rcv.at[4], near(1, 0)).start()
+    send_rows(0, 4)
+    rows_to_columns(0, 4, 5)
 
     moments = merge(end_level(a1x, 2), float(2 * PIX))
     start_level(z_g, a1z, 3, moments)
-
-    waiter(rh_r, 4).wait()
-    ext[:, 2 + TILE : 4 + TILE, LEFT : LEFT + TILE, :] = rh_r[0]
-    ext[:, 0:2, LEFT : LEFT + TILE, :] = rh_r[1]
-    for a in range(2):
-        for k in range(2):
-            ch_s[0, a, k, 0:ROWS, :] = ext[a, :, LEFT + k, :]
-            ch_s[1, a, k, 0:ROWS, :] = ext[a, :, LEFT + TILE - 2 + k, :]
-    remote(ch_s.at[0], ch_r.at[0], snd.at[5], rcv.at[5], near(0, -1)).start()
-    remote(ch_s.at[1], ch_r.at[1], snd.at[5], rcv.at[5], near(0, 1)).start()
-    waiter(ch_r, 5).wait()
-    for a in range(2):
-        for k in range(2):
-            ext[a, :, LEFT + TILE + k, :] = ch_r[0, a, k, 0:ROWS, :]
-            ext[a, :, LEFT - 2 + k, :] = ch_r[1, a, k, 0:ROWS, :]
+    put_columns(1, 28)
 
     row_lo = jnp.where(row == 0, 2, 0)
     row_hi = jnp.where(row == n_row - 1, 2 + TILE, ROWS)
@@ -429,6 +451,7 @@
         t2[pl.ds(first, 17)] = dot_nt(windows(x3c, first, 17), wt2[...]).reshape(17, WIDE, CH)
 
     loop(2, cot_conv)
+    put_columns(0, 5)
 
     moments = merge(end_level(a1z, 3), float(2 * n_xy * PIX))
     mean_ch = moments[0:1]
@@ -462,27 +485,25 @@
 
     loop(2, hidden_rows)
 
-    def tap_grads(x3, gi, half, us):
+    def tap_grads(half):
         length = (ROWS - 2) * WIDE
         grad = jnp.concatenate(
-            [gi[2 - u : 2 - u + ROWS - 2].reshape(length, CH) for u in us], axis=1
+            [gi[half, 2 - u : 2 - u + ROWS - 2].reshape(length, CH) for u in range(3)], axis=1
         )
-        out = dot_tn(x3[1 : ROWS - 1].reshape(length, 3 * CH), grad)
-        for n, u in enumerate(us):
+        out = dot_tn(x3ab[half, 1 : ROWS - 1].reshape(length, 3 * CH), grad)
+        for u in range(3):
             for v in range(3):
                 to, first = (glong, 3 * u + v) if u < 2 else (gshort, v)
                 to[half, first * CH : (first + 1) * CH, :] = out[
-                    v * CH : (v + 1) * CH, n * CH : (n + 1) * CH
+                    v * CH : (v + 1) * CH, u * CH : (u + 1) * CH
                 ]
 
-    tap_grads(x3b, gic, 0, (0, 1))
-    tap_grads(x3a, gig, 1, (0, 1))
+    tap_grads(1 - core)
     swap_long = remote(glong.at[1 - core], clong, snd.at[6], rcv.at[6], core_dev)
     swap_long.start()
-    tap_grads(x3b, gic, 0, (2,))
-    tap_grads(x3a, gig, 1, (2,))
     swap_short = remote(gshort.at[1 - core], cshort, snd.at[7], rcv.at[7], core_dev)
     swap_short.start()
+    tap_grads(core)
 
     inner = slice(LEFT, LEFT + TILE)
     written = []
@@ -495,8 +516,6 @@
         first = 2 + i * 16
         out = dot(windows(x3b, first, 16), w2[...].reshape(HALF, CH)).reshape(16, WIDE, CH)
         feat[pl.ds(i * 16, 16)] = (ext[0, pl.ds(first, 16), inner, :] + out[:, inner, :]).astype(BF16)
-
-    out_rows(0)
 
     def share_out(mine, theirs, to, landing, k):
         def add(m, carry):
@@ -558,6 +577,7 @@
     m_swap = remote(msend.at[1 - core], mrecv, snd.at[13], rcv.at[13], core_dev)
     m_swap.start()
 
+    out_rows(0)
     out_rows(1)
     write_out(feat, feat_hbm)
 
@@ -583,21 +603,25 @@
     long_rows = glong.shape[1] // n_xy
     long_tiles = long_rows // 8
     tiles = zsrc.shape[0] // 8
+    spare = tiles - 1
     turn = (xy + 8 * core) & (n_z - 1)
-    mine = (z - turn) & (n_z - 1)
+    own = (z - turn) & (n_z // 2 - 1)
+    twice = own == 0
 
     def send_tile(t, carry):
-        goal = (t + turn) & (n_z - 1)
-
-        @pl.when(goal != z)
-        def _():
-            remote(
-                zsrc.at[pl.ds(pl.multiple_of(t * 8, 8), 8)],
-                zb.at[z],
-                snd.at[16],
-                rcv.at[16],
-                member_of(z_g, at, goal),
-            ).start()
+        for half in range(2):
+            goal = (t + turn + half * n_z // 2) & (n_z - 1)
+            slot = jnp.where(t == spare, 1, 0)
+
+            @pl.when(goal != z)
+            def _():
+                remote(
+                    zsrc.at[pl.ds(pl.multiple_of(t * 8, 8), 8)],
+                    zb.at[slot, z],
+                    snd.at[16],
+                    rcv.at[jnp.where(t == spare, 26, 16)],
+                    member_of(z_g, at, goal),
+                ).start()
 
         return carry
 
@@ -615,29 +639,34 @@
         waiter(mxy.at[pl.ds(0, n_xy - 1)], 14).wait_recv()
         start_level(z_g, mz, 15, add_up([mxy[i] for i in range(n_xy)]))
 
-    spot = pl.ds(pl.multiple_of(jnp.minimum(mine, tiles - 1) * 8, 8), 8)
-
-    def whole_tile(k):
-        zb[z] = zsrc[spot, :]
-        waiter(zb.at[pl.ds(0, n_z - 1)], 16).wait_recv()
-        zres[spot, :] = add_up([zb[i] for i in range(n_z)]) * report
-
-        def send(device, m):
-            remote(zres.at[spot], zres.at[spot], snd.at[17], rcv.at[k], device).start()
-
-        each_other(z_g, at, send)
-
-    in_long = mine < long_tiles
-    in_short = (mine >= long_tiles) & (mine < tiles)
-    owner = mine < tiles
+    def whole_tile(slot, tile, k_in, k_out):
+        spot = pl.ds(pl.multiple_of(tile * 8, 8), 8)
+        zb[slot, z] = zsrc[spot, :]
+        waiter(zb.at[slot, pl.ds(0, n_z - 1)], k_in).wait_recv()
+        zres[spot, :] = add_up([zb[slot, i] for i in range(n_z)]) * report
+
+        def send(k, carry):
+            away = (k + 1) >> 1
+            goal = z + jnp.where((k & 1) == 1, n_z // 4 - away, away - n_z // 4)
+            device = member_of(z_g, at, (goal + n_z) & (n_z - 1))
+            remote(zres.at[spot], zres.at[spot], snd.at[17], rcv.at[k_out], device).start()
+            return carry
+
+        lax.fori_loop(0, n_z // 2 - 1, send, 0)
+
+    in_long = own < long_tiles
 
     @pl.when(in_long)
     def _():
-        whole_tile(17)
-
-    @pl.when(in_short)
+        whole_tile(0, own, 16, 17)
+
+    @pl.when(jnp.logical_not(in_long))
     def _():
-        whole_tile(18)
+        whole_tile(0, own, 16, 18)
+
+    @pl.when(twice)
+    def _():
+        whole_tile(1, spare, 26, 18)
 
     totals = add_up(end_level(a2z, 12))
     ggain[...] = totals[1:2] * report
@@ -682,12 +711,12 @@
 
             each_other(xy_g, at, send)
 
-    def wait_tiles(count, mine_too, k):
-        @pl.when(mine_too)
+    def wait_tiles(count, some_mine, k):
+        @pl.when(some_mine)
         def _():
             waiter(zres.at[pl.ds(0, (count - 1) * 8)], k).wait_recv()
 
-        @pl.when(jnp.logical_not(mine_too))
+        @pl.when(jnp.logical_not(some_mine))
         def _():
             waiter(zres.at[pl.ds(0, count * 8)], k).wait_recv()
 
@@ -702,7 +731,7 @@
     wait_tiles(long_tiles, in_long, 17)
     long_out[core, xy] = zres[0:long_rows].astype(BF16)
     send_shares(long_out, 21)
-    wait_tiles(tiles - long_tiles, in_short, 18)
+    wait_tiles(tiles - long_tiles, jnp.logical_not(in_long) | twice, 18)
     rest = zres[long_rows:]
     short_out[core, xy] = jnp.concatenate([rest, jnp.zeros((short_out.shape[2] - rest.shape[0], CH), F32)], axis=0).astype(BF16)
     send_shares(short_out, 22)
@@ -780,14 +809,18 @@
     def _():
         waiter(mown, 14).wait_send()
 
-    @pl.when(owner)
+    once = n_z // 2 - 1
+    waiter(zsrc, 16).wait_send()
+    waiter(zb.at[0, pl.ds(0, once)], 17).wait_send()
+
+    @pl.when(twice)
+    def _():
+        waiter(zsrc.at[pl.ds(0, (tiles - 2) * 8)], 16).wait_send()
+        waiter(zb.at[0, pl.ds(0, once)], 17).wait_send()
+
+    @pl.when(jnp.logical_not(twice))
     def _():
         waiter(zsrc.at[pl.ds(0, (tiles - 1) * 8)], 16).wait_send()
-        waiter(zb.at[pl.ds(0, n_z - 1)], 17).wait_send()
-
-    @pl.when(jnp.logical_not(owner))
-    def _():
-        waiter(zsrc, 16).wait_send()
 
     back_long.wait()
     widen_long(1 - core)
@@ -865,12 +898,10 @@
         pltpu.VMEM((2, 2, 2, TILE, CH), F32),
         pltpu.VMEM((2, 2, 2, 40, CH), F32),
         pltpu.VMEM((2, 2, 2, 40, CH), F32),
+        pltpu.VMEM((2, ROWS, WIDE, 3 * CH), BF16),
         pltpu.VMEM((ROWS, WIDE, 3 * CH), BF16),
         pltpu.VMEM((ROWS, WIDE, 3 * CH), BF16),
-        pltpu.VMEM((ROWS, WIDE, 3 * CH), BF16),
-        pltpu.VMEM((ROWS, WIDE, 3 * CH), BF16),
-        pltpu.VMEM((ROWS, WIDE, CH), BF16),
-        pltpu.VMEM((ROWS, WIDE, CH), BF16),
+        pltpu.VMEM((2, ROWS, WIDE, CH), BF16),
         pltpu.VMEM((ROWS, WIDE, CH), F32),
         pltpu.VMEM((TILE, TILE, CH), F32),
         pltpu.VMEM((PIX, 4 * CH), BF16),
@@ -903,13 +934,13 @@
         pltpu.VMEM((n_xy, rows_long, CH), F32),
         pltpu.VMEM((n_xy, rows_short, CH), F32),
         pltpu.VMEM((rows_long + rows_short, CH), F32),
-        pltpu.VMEM((n_z, 8, CH), F32),
+        pltpu.VMEM((2, n_z, 8, CH), F32),
         pltpu.VMEM((rows_long + rows_short, CH), F32),
         pltpu.VMEM((9, 2, 24, CH), F32),
         pltpu.VMEM((9, 2, 24, CH), F32),
         pltpu.SemaphoreType.DMA((19,)),
-        pltpu.SemaphoreType.DMA((26,)),
-        pltpu.SemaphoreType.DMA((26,)),
+        pltpu.SemaphoreType.DMA((29,)),
+        pltpu.SemaphoreType.DMA((29,)),
     ]
     parts = pl.pallas_call(
         body,

time: 78.2 us -> 73.6 us (0.941)
  Pallas kernels: 77.4 us -> 72.8 us
    pallas_call x1, Pallas kernels: 75.2 us -> 70.5 us  [shards(): pl.pallas_call(body, out_shape=results, in_specs=[hbm] * 10, out_specs=[h...]
where the time goes in v3:
time: 73.6 us; the launch traced here: 73.4 us
  Pallas kernels  72.8 us (99%)
    pallas_call x1, Pallas kernels, shards(): pl.pallas_call(body, out_shape=results, in_specs=[hbm] * 10, out_specs=[h...  70.5 us
    pallas_call x1, Pallas kernels, shards(): pl.pallas_call(finish, out_shape=outputs, in_specs=[hbm] * 6, out_specs=[...  2.29 us

profile of v3, /device:TPU:1, one launch (start us, length us, event | category | flops | bytes accessed | tf_op | source)
XLA Modules:
  0.0 73.4 jit_solution(1856318132451469473)
XLA Ops:
  0.6 70.5 %block.1 = (bf16[32,32,128]{2,1,0:T(8,128)(2,1)}, f32[20,2,128]{2,1,0:T(2,128)}, f32[2,1152,128]{2,1,0:T(8,128)}, f32[20,128]{1,0:T(8,128)}, f32[1,128]{1,0:T(1,128)}, /*index=5*/f32[1,128]{1,0:T(1,128)}) custom-call(bf16[20,2,128]{2,1,0:T(2,128)(2,1)} %bitcast.12, s32[1,1,6]{2,1,0:T(1,128)} %refs_1_.1, s32[1,1,6]{2,1,0:T(1,128)} %refs_2_.1, ...), custom_call_target="tpu_custom_call" | custom-call | tf_op jit(solution)/shard_map/block/pallas_call | solution.py:945
  71.2 2.3 %finish.1 = (f32[1152,128]{1,0:T(8,128)}, f32[1152,128]{1,0:T(8,128)}, bf16[32,32,128]{2,1,0:T(8,128)(2,1)}, f32[20,2,128]{2,1,0:T(2,128)}, f32[20,128]{1,0:T(8,...) custom-call(bf16[32,32,128]{2,1,0:T(8,128)(2,1)} %get-tuple-element.20.feat, f32[20,2,128]{2,1,0:T(2,128)} %get-tuple-element.21.gcoarse, ...), custom_call_target="tpu_custom_call" | custom-call | tf_op jit(solution)/shard_map/finish/pallas_call | solution.py:969

commit v4 on v3

--- a/solution.py
+++ b/solution.py
@@ -131,12 +131,12 @@
     w1_hbm,
     w2_hbm,
     cot_hbm,
-    feat_hbm,
-    gcoarse_hbm,
-    grads_hbm,
-    glift_hbm,
-    gland_hbm,
-    ggain_hbm,
+    feat,
+    gcoarse,
+    grads,
+    glift,
+    gland,
+    ggain,
     coarse,
     ids,
     quad,
@@ -149,6 +149,8 @@
     up,
     ft,
     wext,
+    wpair,
+    upt,
     w1,
     w2,
     cotv,
@@ -172,12 +174,6 @@
     a2c,
     a2x,
     a2z,
-    feat,
-    gcoarse,
-    grads,
-    glift,
-    gland,
-    ggain,
     long_out,
     short_out,
     msend,
@@ -202,6 +198,7 @@
     dma,
     snd,
     rcv,
+    answers,
 ):
     row = lax.axis_index("row")
     col = lax.axis_index("col")
@@ -238,8 +235,16 @@
     for dr, dc in around:
         if (dr, dc) != (0, 0):
             greet(near(dr, dc), 0)
-    for group in (core_g, xy_g, z_g):
+    for group in (core_g, xy_g):
         each_other(group, at, greet)
+
+    def along_z(away):
+        return member_of(z_g, at, (z + away + n_z) & (n_z - 1))
+
+    quarter = n_z // 4
+    for away in range(quarter, 0, -1):
+        greet(along_z(away), 0)
+        greet(along_z(-away), 0)
 
     pairs = [
         (coarse_hbm, coarse),
@@ -265,11 +270,14 @@
     padf[2, 0:CIN, :] = lift_w[...].astype(F32)
     cand[4] = padf[0:2].astype(BF16)
 
-    pl.semaphore_wait(barrier, 8 + 1 + n_xy - 1 + n_z - 1)
+    pl.semaphore_wait(barrier, 8 + 1 + n_xy - 1 + 2 * quarter)
 
     for s, (dr, dc) in enumerate(around):
         if s != 4:
             remote(cand.at[4], cand.at[8 - s], snd.at[0], rcv.at[0], near(dr, dc)).start()
+
+    for away in (quarter, -quarter):
+        pl.semaphore_signal(answers, inc=1, device_id=along_z(away), device_id_type=MESH)
 
     for load in loads[2:]:
         load.wait()
@@ -298,6 +306,11 @@
         return jnp.maximum(1.0 - jnp.abs(where - cell_at.astype(F32)), 0.0)
 
     up[...] = (hat(fine >> 5, cell >> 4, 8) * hat(fine & 31, cell & 15, 16)).astype(BF16)
+    fine = lax.broadcasted_iota(jnp.int32, (512, CH), 0)
+    cell = lax.broadcasted_iota(jnp.int32, (512, CH), 1)
+    turned = (hat(fine >> 5, cell >> 4, 8) * hat(fine & 31, cell & 15, 16)).astype(BF16)
+    for k in range(3):
+        upt[:, k * CH : (k + 1) * CH] = turned
 
     pix = lax.broadcasted_iota(jnp.int32, (TILE, PIX), 1)
     line = lax.broadcasted_iota(jnp.int32, (TILE, PIX), 0)
@@ -305,9 +318,14 @@
     lines = dot(land[...].astype(F32).astype(BF16), spread)
     lines = jnp.where((pix >> 5) == line, lines, 0.0).astype(BF16)
     wext[0:32] = padf[2].astype(BF16)
+    wpair[...] = jnp.zeros_like(wpair)
+    wpair[0, 0:32] = wext[0:32]
+    wpair[1, 32:64] = wext[0:32]
     for k, part in enumerate(split_three(jnp.broadcast_to(land_v[...], (32, CH)))):
         ft[32 * (k + 1) : 32 * (k + 2), :] = lines
         wext[32 * (k + 1) : 32 * (k + 2), :] = part
+    on_land = dot_tn(ft[32:], wext[32:])
+    ext[0, 2 : 2 + TILE, LEFT : LEFT + TILE, :] = on_land.reshape(TILE, TILE, CH)
 
     for lo, hi in ((0, LEFT), (LEFT + TILE, WIDE)):
         ext[:, :, lo:hi, :] = jnp.zeros((2, ROWS, 8, CH), F32)
@@ -355,11 +373,14 @@
                 total = total + weight[q, s, m] * cand[s, m].astype(F32)
         sums.append(total)
     parts = split_three(jnp.concatenate(sums, axis=0))
-    raised = dot(jnp.concatenate(parts, axis=0), up[...])
-    raised = raised[0:64] + raised[64:128] + raised[128:192]
-    ft[0:32, 0:512] = raised[0:32].astype(BF16)
-    ft[0:32, 512:1024] = raised[32:64].astype(BF16)
-    lifted = dot_tn(ft[...], wext[...])
+    raised = dot_nt(upt[...], jnp.concatenate(parts, axis=1)).astype(BF16)
+    lifted = jnp.concatenate(
+        [
+            dot(raised, wpair[q]) + ext[0, 2 + 16 * q : 18 + 16 * q, LEFT : LEFT + TILE, :].reshape(512, CH)
+            for q in range(2)
+        ],
+        axis=0,
+    )
     ext[0, 2 : 2 + TILE, LEFT : LEFT + TILE, :] = lifted.reshape(TILE, TILE, CH)
     mean_here = jnp.sum(lifted, axis=0, keepdims=True) * (1.0 / PIX)
     apart = lifted - mean_here
@@ -393,6 +414,10 @@
 
     pack_rows(0)
     rows_to_columns(1, 27, 28)
+    by_field = dot(jnp.concatenate(parts, axis=0), up[...])
+    by_field = by_field[0:64] + by_field[64:128] + by_field[128:192]
+    ft[0:32, 0:512] = by_field[0:32].astype(BF16)
+    ft[0:32, 512:1024] = by_field[32:64].astype(BF16)
 
     moments = merge(end_level(a1c, 1), float(PIX))
     start_level(xy_g, a1x, 2, moments)
@@ -400,6 +425,7 @@
     rows_to_columns(0, 4, 5)
 
     moments = merge(end_level(a1x, 2), float(2 * PIX))
+    pl.semaphore_wait(answers, 2)
     start_level(z_g, a1z, 3, moments)
     put_columns(1, 28)
 
@@ -506,11 +532,6 @@
     tap_grads(core)
 
     inner = slice(LEFT, LEFT + TILE)
-    written = []
-
-    def write_out(src, dst):
-        written.append(pltpu.make_async_copy(src, dst, dma.at[10 + len(written)]))
-        written[-1].start()
 
     def out_rows(i):
         first = 2 + i * 16
@@ -566,20 +587,19 @@
     lane = lax.broadcasted_iota(jnp.int32, (24, CH), 1)
     field_rows = dot(ft[...], glb[...])
 
-    def by_field(k):
+    def field_sums(k):
         part = field_rows[:, k * CH : (k + 1) * CH] + field_rows[:, (k + 1) * CH : (k + 2) * CH]
         on_land = jnp.sum(part[32:64], axis=0, keepdims=True)
         return jnp.where(which == CIN, on_land, part[0:24])
 
     alone = dot_nt(jnp.full((8, PIX), 1.0, BF16), ft[...])[0:1]
-    msend[0] = by_field(0)
-    msend[1] = jnp.where(which == CIN + 1, alone, by_field(2))
+    msend[0] = field_sums(0)
+    msend[1] = jnp.where(which == CIN + 1, alone, field_sums(2))
     m_swap = remote(msend.at[1 - core], mrecv, snd.at[13], rcv.at[13], core_dev)
     m_swap.start()
 
     out_rows(0)
     out_rows(1)
-    write_out(feat, feat_hbm)
 
     start_level(xy_g, a2x, 11, add_up(end_level(a2c, 10)))
 
@@ -670,7 +690,6 @@
 
     totals = add_up(end_level(a2z, 12))
     ggain[...] = totals[1:2] * report
-    write_out(ggain, ggain_hbm)
     plain_sum = group_sums(totals[0:1] * gain) * (1.0 / members)
     cross_sum = group_sums(totals[1:2] * gain) * (1.0 / members)
 
@@ -743,7 +762,6 @@
             if s != 4:
                 total = total + ret_r[s, m]
         gcoarse[:, m, :] = total[0:CIN]
-    write_out(gcoarse, gcoarse_hbm)
 
     @pl.when(holder)
     def _():
@@ -761,14 +779,10 @@
 
     def widen_long(half):
         grads[half, 0:long_all, :] = long_out[half].astype(F32).reshape(long_all, CH)
-        piece = (half, pl.ds(0, long_all))
-        write_out(grads.at[piece], grads_hbm.at[piece])
 
     def widen_short(half):
         part = short_out[half][:, 0:short_rows, :].astype(F32)
         grads[half, long_all:, :] = part.reshape(n_xy * short_rows, CH)
-        piece = (half, pl.ds(long_all, n_xy * short_rows))
-        write_out(grads.at[piece], grads_hbm.at[piece])
 
     waiter(long_out.at[core, pl.ds(0, n_xy - 1)], 21).wait_recv()
     back_long = remote(long_out.at[core], long_out.at[core], snd.at[24], rcv.at[24], core_dev)
@@ -783,8 +797,6 @@
     lift_all = lift_all * report
     glift[...] = lift_all[0:CIN]
     gland[...] = lift_all[CIN : CIN + 1]
-    write_out(glift, glift_hbm)
-    write_out(gland, gland_hbm)
 
     waiter(short_out.at[core, pl.ds(0, n_xy - 1)], 22).wait_recv()
     back_short = remote(short_out.at[core], short_out.at[core], snd.at[25], rcv.at[25], core_dev)
@@ -826,19 +838,13 @@
     widen_long(1 - core)
     back_short.wait()
     widen_short(1 - core)
-    for copy in written:
-        copy.wait()
 
 
 def finish(feat, gcoarse, grads, glift, gland, ggain, *rest):
-    outs, held, dma = rest[:7], rest[7:14], rest[14]
+    outs, dma = rest[:7], rest[7]
     sources = (grads.at[1], grads.at[0], feat, gcoarse, glift, gland, ggain)
-    ins = [pltpu.make_async_copy(a, b, dma.at[0, k]) for k, (a, b) in enumerate(zip(sources, held))]
-    for copy in ins:
-        copy.start()
-    copies = [pltpu.make_async_copy(a, b, dma.at[1, k]) for k, (a, b) in enumerate(zip(held, outs))]
-    for arrived, copy in zip(ins, copies):
-        arrived.wait()
+    copies = [pltpu.make_async_copy(a, b, dma.at[k]) for k, (a, b) in enumerate(zip(sources, outs))]
+    for copy in copies:
         copy.start()
     for copy in copies:
         copy.wait()
@@ -864,6 +870,7 @@
         kernel(n_row, n_col, *refs)
 
     hbm = pl.BlockSpec(memory_space=pltpu.HBM)
+    vmem = pl.BlockSpec(memory_space=pltpu.VMEM)
     rows_long = 6 * CH // n_xy
     rows_short = 3 * CH // n_xy
     pad_short = -(-rows_short // 16) * 16
@@ -888,6 +895,8 @@
         pltpu.VMEM((CH, 512), BF16),
         pltpu.VMEM((CH, PIX), BF16),
         pltpu.VMEM((CH, CH), BF16),
+        pltpu.VMEM((2, 64, CH), BF16),
+        pltpu.VMEM((512, 3 * CH), BF16),
         pltpu.VMEM((TAPS, CH, CH), BF16),
         pltpu.VMEM((TAPS, CH, CH), BF16),
         pltpu.VMEM((TILE, TILE, CH), BF16),
@@ -911,12 +920,6 @@
         pltpu.VMEM((2, 2, CH), F32),
         pltpu.VMEM((n_xy, 2, CH), F32),
         pltpu.VMEM((n_z, 2, CH), F32),
-        pltpu.VMEM((TILE, TILE, CH), BF16),
-        pltpu.VMEM((CIN, 2, CH), F32),
-        pltpu.VMEM((2, HALF, CH), F32),
-        pltpu.VMEM((CIN, CH), F32),
-        pltpu.VMEM((1, CH), F32),
-        pltpu.VMEM((1, CH), F32),
         pltpu.VMEM((2, n_xy, rows_long, CH), BF16),
         pltpu.VMEM((2, n_xy, pad_short, CH), BF16),
         pltpu.VMEM((2, 24, CH), F32),
@@ -938,42 +941,47 @@
         pltpu.VMEM((rows_long + rows_short, CH), F32),
         pltpu.VMEM((9, 2, 24, CH), F32),
         pltpu.VMEM((9, 2, 24, CH), F32),
-        pltpu.SemaphoreType.DMA((19,)),
+        pltpu.SemaphoreType.DMA((10,)),
         pltpu.SemaphoreType.DMA((29,)),
         pltpu.SemaphoreType.DMA((29,)),
+        pltpu.SemaphoreType.REGULAR,
     ]
     parts = pl.pallas_call(
         body,
         out_shape=results,
         in_specs=[hbm] * 10,
-        out_specs=[hbm] * 6,
+        out_specs=[vmem] * 6,
         scratch_shapes=scratch,
         compiler_params=pltpu.CompilerParams(
-            collective_id=0, has_side_effects=True, vmem_limit_bytes=60 << 20
+            collective_id=0, has_side_effects=True, vmem_limit_bytes=44 << 20
         ),
         name="block",
     )(
-        jnp.transpose(coarse_blocks[0, 0], (1, 0, 2)),
-        block_ids,
-        quadrant,
-        land_mask,
-        lift_weight,
-        land_vector.reshape(1, CH),
-        norm_gain.reshape(1, CH),
-        first_weight,
-        second_weight,
-        cotangent,
+        *(
+            pltpu.with_memory_space_constraint(operand, pltpu.HBM)
+            for operand in (
+                jnp.transpose(coarse_blocks[0, 0], (1, 0, 2)),
+                block_ids,
+                quadrant,
+                land_mask,
+                lift_weight,
+                land_vector.reshape(1, CH),
+                norm_gain.reshape(1, CH),
+                first_weight,
+                second_weight,
+                cotangent,
+            )
+        )
     )
     wide = jax.ShapeDtypeStruct((HALF, CH), F32)
     outputs = [wide, wide, results[0], results[1]] + results[3:]
     grad_first, grad_second, features, grad_coarse, grad_lift, grad_land, grad_gain = pl.pallas_call(
         finish,
         out_shape=outputs,
-        in_specs=[hbm] * 6,
+        in_specs=[vmem] * 6,
         out_specs=[hbm] * 7,
-        scratch_shapes=[pltpu.VMEM(out.shape, out.dtype) for out in outputs]
-        + [pltpu.SemaphoreType.DMA((2, 7))],
-        compiler_params=pltpu.CompilerParams(vmem_limit_bytes=60 << 20),
+        scratch_shapes=[pltpu.SemaphoreType.DMA((7,))],
+        compiler_params=pltpu.CompilerParams(vmem_limit_bytes=16 << 20),
         name="finish",
     )(*parts)
     return (

time: 73.6 us -> 69.6 us (0.946)
  Pallas kernels: 72.8 us -> 68.8 us
    pallas_call x2, Pallas kernels: 72.8 us -> 68.8 us  [the longest x1 67.6 us: shards(): pl.pallas_call(body, out_shape=results, in_specs=[hbm] * 10, out_specs=[v...]
where the time goes in v4:
time: 69.6 us; the launch traced here: 69.4 us
  Pallas kernels  68.8 us (99%)
    pallas_call x1, Pallas kernels, shards(): pl.pallas_call(body, out_shape=results, in_specs=[hbm] * 10, out_specs=[v...  67.6 us

profile of v4, /device:TPU:1, one launch (start us, length us, event | category | flops | bytes accessed | tf_op | source)
XLA Modules:
  0.0 69.4 jit_solution(12061917545691519514)
XLA Ops:
  0.6 67.6 %block.1 = (bf16[32,32,128]{2,1,0:T(8,128)(2,1)S(1)}, f32[20,2,128]{2,1,0:T(2,128)S(1)}, f32[2,1152,128]{2,1,0:T(8,128)S(1)}, f32[20,128]{1,0:T(8,128)S(1)}, f32[1,128]{1,0:T(1,128)S(1)}, /*index=5*/f32[1,128]{1,0:T(1,128)S(1)}) custom-call(bf16[20,2,128]{2,1,0:T(2,128)(2,1)} %bitcast.12, s32[1,1,6]{2,1,0:T(1,128)} %refs_1_.1, s32[1,1,6]{2,1,0:T(1,128)} %refs_2_.1, ...), custom_call_target="tpu_custom_call" | custom-call | tf_op jit(solution)/shard_map/block/pallas_call | solution.py:949
  68.2 1.2 %finish.1 = (f32[1152,128]{1,0:T(8,128)}, f32[1152,128]{1,0:T(8,128)}, bf16[32,32,128]{2,1,0:T(8,128)(2,1)}, f32[20,2,128]{2,1,0:T(2,128)}, f32[20,128]{1,0:T(8,...) custom-call(bf16[32,32,128]{2,1,0:T(8,128)(2,1)S(1)} %get-tuple-element.20.feat, f32[20,2,128]{2,1,0:T(2,128)S(1)} %get-tuple-element.21.gcoarse, ...), custom_call_target="tpu_custom_call" | custom-call | tf_op jit(solution)/shard_map/finish/pallas_call | solution.py:978

commit v5 on v4

--- a/solution.py
+++ b/solution.py
@@ -755,6 +755,19 @@
     short_out[core, xy] = jnp.concatenate([rest, jnp.zeros((short_out.shape[2] - rest.shape[0], CH), F32)], axis=0).astype(BF16)
     send_shares(short_out, 22)
 
+    long_all = n_xy * long_rows
+    short_rows = zsrc.shape[0] - long_rows
+
+    def widen_long(half):
+        grads[half, 0:long_all, :] = long_out[half].astype(F32).reshape(long_all, CH)
+
+    def widen_short(half):
+        part = short_out[half][:, 0:short_rows, :].astype(F32)
+        grads[half, long_all:, :] = part.reshape(n_xy * short_rows, CH)
+
+    waiter(long_out.at[core, pl.ds(0, n_xy - 1)], 21).wait_recv()
+    back_long = remote(long_out.at[core], long_out.at[core], snd.at[24], rcv.at[24], core_dev)
+    back_long.start()
     waiter(ret_r.at[pl.ds(0, 8)], 19).wait()
     for m in range(2):
         total = ret_s[4, m]
@@ -773,21 +786,12 @@
 
     m_back = remote(mall.at[core], mall.at[core], snd.at[23], rcv.at[23], core_dev)
     m_back.start()
-
-    long_all = n_xy * long_rows
-    short_rows = zsrc.shape[0] - long_rows
-
-    def widen_long(half):
-        grads[half, 0:long_all, :] = long_out[half].astype(F32).reshape(long_all, CH)
-
-    def widen_short(half):
-        part = short_out[half][:, 0:short_rows, :].astype(F32)
-        grads[half, long_all:, :] = part.reshape(n_xy * short_rows, CH)
-
-    waiter(long_out.at[core, pl.ds(0, n_xy - 1)], 21).wait_recv()
-    back_long = remote(long_out.at[core], long_out.at[core], snd.at[24], rcv.at[24], core_dev)
-    back_long.start()
     widen_long(core)
+
+    waiter(short_out.at[core, pl.ds(0, n_xy - 1)], 22).wait_recv()
+    back_short = remote(short_out.at[core], short_out.at[core], snd.at[25], rcv.at[25], core_dev)
+    back_short.start()
+    widen_short(core)
 
     m_back.wait()
     straight, crossed = mall[0], mall[1]
@@ -797,11 +801,6 @@
     lift_all = lift_all * report
     glift[...] = lift_all[0:CIN]
     gland[...] = lift_all[CIN : CIN + 1]
-
-    waiter(short_out.at[core, pl.ds(0, n_xy - 1)], 22).wait_recv()
-    back_short = remote(short_out.at[core], short_out.at[core], snd.at[25], rcv.at[25], core_dev)
-    back_short.start()
-    widen_short(core)
 
     waiter(cand.at[pl.ds(0, 8)], 0).wait_send()
     swap_long.wait_send()

time: 69.6 us -> 69.6 us (level)
  no operation moved by 1% of the time
where the time goes in v5:
time: 69.6 us; the launch traced here: 69.4 us
  Pallas kernels  68.8 us (99%)
    pallas_call x1, Pallas kernels, shards(): pl.pallas_call(body, out_shape=results, in_specs=[hbm] * 10, out_specs=[v...  67.6 us

profile of v5, /device:TPU:1, one launch (start us, length us, event | category | flops | bytes accessed | tf_op | source)
XLA Modules:
  0.0 69.4 jit_solution(15803403771414702339)
XLA Ops:
  0.6 67.6 %block.1 = (bf16[32,32,128]{2,1,0:T(8,128)(2,1)S(1)}, f32[20,2,128]{2,1,0:T(2,128)S(1)}, f32[2,1152,128]{2,1,0:T(8,128)S(1)}, f32[20,128]{1,0:T(8,128)S(1)}, f32[1,128]{1,0:T(1,128)S(1)}, /*index=5*/f32[1,128]{1,0:T(1,128)S(1)}) custom-call(bf16[20,2,128]{2,1,0:T(2,128)(2,1)} %bitcast.12, s32[1,1,6]{2,1,0:T(1,128)} %refs_1_.1, s32[1,1,6]{2,1,0:T(1,128)} %refs_2_.1, ...), custom_call_target="tpu_custom_call" | custom-call | tf_op jit(solution)/shard_map/block/pallas_call | solution.py:948
  68.2 1.2 %finish.1 = (f32[1152,128]{1,0:T(8,128)}, f32[1152,128]{1,0:T(8,128)}, bf16[32,32,128]{2,1,0:T(8,128)(2,1)}, f32[20,2,128]{2,1,0:T(2,128)}, f32[20,128]{1,0:T(8,...) custom-call(bf16[32,32,128]{2,1,0:T(8,128)(2,1)S(1)} %get-tuple-element.20.feat, f32[20,2,128]{2,1,0:T(2,128)S(1)} %get-tuple-element.21.gcoarse, ...), custom_call_target="tpu_custom_call" | custom-call | tf_op jit(solution)/shard_map/finish/pallas_call | solution.py:977
